TPU v7x, 1024 devices: a whole 4x8x16 slice. The times are simulated.
1024 devices in a mesh: outer: 32 (over y, z_hi), inner: 32 (over z_lo, x, core).
Axes of the slice: x: 4, y: 8, z: 16 (z_hi: 4, z_lo: 4; z = z_hi * 4 + z_lo), core: 2. Of those that a mesh axis runs over, the one named last changes fastest.
Arguments:
- image_embeds: bfloat16 [524288, 512], P(('outer', 'inner')), may hold values from -0.17766058 to 0.17766058
- text_embeds: bfloat16 [524288, 512], P(('outer', 'inner')), may hold values from -0.17766058 to 0.17766058
- image_lse: float32 [524288], P(('outer', 'inner')), as said below
- text_lse: float32 [524288], P(('outer', 'inner')), as said below
- logit_scale: float32 [], replicated, may hold values from 90 to 100, as said below
Outputs:
- image_grad: float32 [524288, 512], P(('outer', 'inner'))
- text_grad: float32 [524288, 512], P(('outer', 'inner'))
Inputs may be any that keep to these rules, and one draw needn't show every extreme that they name: logit_scale is one positive number. `image_lse`: saved by the forward pass: for image row i, the log of the sum of exp(score_ij) over the text rows j that the window pairs with it. `text_lse`: saved by the forward pass: for text row j, the log of the sum of exp(score_ij) over the image rows i that the window pairs with it.
All inputs are finite; a program needn't handle non-finite values.
Results may differ from a plain program's by a relative error of at most 0.0013.
Values may be sent and summed in bfloat16 or wider, within the bound.
No kernel may reach another device: no remote copies, remote signals or barrier semaphores. Data moves between devices by JAX's collectives and lax.ppermute only.
A program may use at most 32 MiB of HBM per device.

v0:
```python
import jax
import jax.numpy as jnp
from jax import lax
from jax.sharding import PartitionSpec as P


def shifted(value, axis, steps):
    count = lax.axis_size(axis)
    pairs = [(source, (source + steps) % count) for source in range(count)]
    return lax.ppermute(value, axis, pairs)


def split_exact(values):
    upper_part = lax.optimization_barrier(values.astype(jnp.bfloat16))
    remainder = values - upper_part.astype(jnp.float32)
    middle = lax.optimization_barrier(remainder.astype(jnp.bfloat16))
    lower_part = (remainder - middle.astype(jnp.float32)).astype(jnp.bfloat16)
    return jnp.stack([upper_part, middle, lower_part])


def join_exact(pieces):
    widened = pieces.astype(jnp.float32)
    return widened[0] + (widened[1] + widened[2])


def tile_weights(images, image_stat, text_rows, text_stat, factor):
    scores = factor * lax.dot_general(
        images, text_rows, (((1,), (1,)), ((), ())), preferred_element_type=jnp.float32
    )
    return (jnp.exp(scores - image_stat[:, None]) + jnp.exp(scores - text_stat[None, :])).astype(
        jnp.bfloat16
    )


def image_side(weights, text_rows):
    return jnp.dot(weights, text_rows, preferred_element_type=jnp.float32)


def text_side(weights, images):
    return lax.dot_general(
        weights, images, (((0,), (0,)), ((), ())), preferred_element_type=jnp.float32
    )


def local(image_embeds, text_embeds, image_lse, text_lse, logit_scale):
    text_pieces = split_exact(text_lse)
    own_weights = tile_weights(image_embeds, image_lse, text_embeds, text_lse, logit_scale)
    image_total = image_side(own_weights, text_embeds)
    own_text = text_side(own_weights, image_embeds)
    near_text, near_pieces = shifted((text_embeds, text_pieces), "inner", 1)
    far_text, far_pieces, both_text, both_pieces = shifted(
        (text_embeds, text_pieces, near_text, near_pieces), "outer", 1
    )
    near_weights = tile_weights(
        image_embeds, image_lse, near_text, join_exact(near_pieces), logit_scale
    )
    far_weights = tile_weights(
        image_embeds, image_lse, far_text, join_exact(far_pieces), logit_scale
    )
    both_weights = tile_weights(
        image_embeds, image_lse, both_text, join_exact(both_pieces), logit_scale
    )
    image_total = (
        image_total
        + image_side(near_weights, near_text)
        + image_side(far_weights, far_text)
        + image_side(both_weights, both_text)
    )
    back_far, back_both = shifted(
        (text_side(far_weights, image_embeds), text_side(both_weights, image_embeds)), "outer", -1
    )
    second_sum = text_side(near_weights, image_embeds) + back_both
    returned = shifted(second_sum, "inner", -1)
    text_total = own_text + back_far + returned
    image_grad = logit_scale * (image_total - 2.0 * text_embeds.astype(jnp.float32))
    text_grad = logit_scale * (text_total - 2.0 * image_embeds.astype(jnp.float32))
    return (image_grad, text_grad)


def solution(mesh):
    return jax.shard_map(
        local,
        mesh=mesh,
        in_specs=(
            P(("outer", "inner"), None),
            P(("outer", "inner"), None),
            P(("outer", "inner")),
            P(("outer", "inner")),
            P(),
        ),
        out_specs=(P(("outer", "inner"), None), P(("outer", "inner"), None)),
        check_vma=False,
    )
```

profile of v0, /device:TPU:118, one launch (start us, length us, event | category | flops | bytes accessed | tf_op | source)
XLA Modules:
  0.0 283.9 jit_solution(12932081255227698823)
XLA Ops:
  0.6 1.9 collective-permute-start
  2.6 0.7 convert_element_type.43
  3.2 0.0 copy-start.2
  3.3 0.7 copy-done.2
  4.0 0.0 copy-start.3
  4.0 7.4 %collective-permute-done = bf16[512,512]{1,0:T(8,128)(2,1)S(1)} collective-permute-done((bf16[512,512]{1,0:T(8,128)(2,1)}, bf16[512,512]{1,0:T(8,128)(2,1)S(1)}, u32[]{:S(2)}, u32[]{:S(2)}) %collective-permute-start) | collective-permute-done | bytes 524320 | tf_op jit(solution)/shard_map/ppermute | solution.py:10
  11.3 10.9 %collective-permute-start.4 = (bf16[512,512]{1,0:T(8,128)(2,1)S(1)}, bf16[512,512]{1,0:T(8,128)(2,1)S(1)}, u32[]{:S(2)}, u32[]{:S(2)}) collective-permute-start(bf16[512,512]{1,0:T(8,128)(2,1)S(1)} %collective-permute-done), channel_id=1, source_target_pairs={{0,32},{32,64},{64,96},{96,128},{128,160},{160,192},{192,224},{224... | collective-permute-start | bytes 1572872 | tf_op jit(solution)/shard_map/ppermute | solution.py:10
  22.3 1.9 collective-permute-start.1
  24.2 10.0 %collective-permute-start.2 = (bf16[512,512]{1,0:T(8,128)(2,1)}, bf16[512,512]{1,0:T(8,128)(2,1)S(1)}, u32[]{:S(2)}, u32[]{:S(2)}) collective-permute-start(bf16[512,512]{1,0:T(8,128)(2,1)} %param.6), channel_id=1, source_target_pairs={{0,32},{32,64},{64,96},{96,128},{128,160},{160,192},{192,224},{224... | collective-permute-start | bytes 1572872 | tf_op jit(solution)/shard_map/ppermute | solution.py:10
  34.2 6.1 %collective-permute-start.3 = (bf16[3,512]{1,0:T(4,128)(2,1)S(1)}, bf16[3,512]{1,0:T(4,128)(2,1)S(1)}, u32[]{:S(2)}, u32[]{:S(2)}) collective-permute-start(bf16[3,512]{1,0:T(4,128)(2,1)S(1)} %pad_maximum_fusion), channel_id=1, source_target_pairs={{0,32},{32,64},{64,96},{96,128},{128,160},{160,192},{192,224},{224... | collective-permute-start | bytes 9224 | tf_op jit(solution)/shard_map/ppermute | solution.py:10
  41.0 0.0 copy-start
  41.0 0.0 collective-permute-done.1
  41.0 2.1 collective-permute-start.5
  43.1 0.0 copy-done.3
  43.1 1.8 add_convert_fusion.3
  44.9 49.0 %collective-permute-done.5 = bf16[3,512]{1,0:T(4,128)(2,1)S(1)} collective-permute-done((bf16[3,512]{1,0:T(4,128)(2,1)S(1)}, bf16[3,512]{1,0:T(4,128)(2,1)S(1)}, u32[]{:S(2)}, u32[]{:S(2)}) %collective-permute-start.5) | collective-permute-done | bytes 3104 | tf_op jit(solution)/shard_map/ppermute | solution.py:10
  93.9 0.0 collective-permute-done.4
  93.9 0.0 copy-done
  93.9 0.6 add_convert_fusion
  94.6 0.5 fusion.11
  95.1 4.1 %collective-permute-start.7 = (f32[512,512]{1,0:T(8,128)S(1)}, f32[512,512]{1,0:T(8,128)S(1)}, u32[]{:S(2)}, u32[]{:S(2)}) collective-permute-start(f32[512,512]{1,0:T(8,128)S(1)} %fusion.11), channel_id=1, source_target_pairs={{0,992},{32,0},{64,32},{96,64},{128,96},{160,128},{192,160},{224,1... | collective-permute-start | bytes 3145736 | tf_op jit(solution)/shard_map/ppermute | solution.py:10
  99.2 0.0 collective-permute-done.3
  99.3 0.0 collective-permute-done.2
  99.3 0.6 add_convert_fusion.1
  99.9 0.5 fusion.10
  100.4 2.5 collective-permute-start.6
  102.9 0.6 add_convert_fusion.2
  103.5 0.0 copy-start.1
  103.5 23.7 %collective-permute-done.7 = f32[512,512]{1,0:T(8,128)S(1)} collective-permute-done((f32[512,512]{1,0:T(8,128)S(1)}, f32[512,512]{1,0:T(8,128)S(1)}, u32[]{:S(2)}, u32[]{:S(2)}) %collective-permute-start.7) | collective-permute-done | bytes 1048608 | tf_op jit(solution)/shard_map/ppermute | solution.py:10
  127.2 0.5 convolution_add_fusion
  127.7 1.9 collective-permute-start.8
  129.6 0.0 copy-done.1
  129.6 0.4 fusion.9
  130.1 0.4 convolution_add_fusion.4
  130.5 0.4 convolution_add_fusion.3
  131.0 1.4 fusion.4
  132.4 150.0 %collective-permute-done.6 = f32[512,512]{1,0:T(8,128)S(1)} collective-permute-done((f32[512,512]{1,0:T(8,128)S(1)}, f32[512,512]{1,0:T(8,128)S(1)}, u32[]{:S(2)}, u32[]{:S(2)}) %collective-permute-start.6) | collective-permute-done | bytes 1048608 | tf_op jit(solution)/shard_map/ppermute | solution.py:10
  282.4 0.0 collective-permute-done.8
  282.4 1.5 fusion.2
  (12 shorter events, 0.1 us)
Async XLA Ops:
  0.6 10.7 %collective-permute-start = (bf16[512,512]{1,0:T(8,128)(2,1)}, bf16[512,512]{1,0:T(8,128)(2,1)S(1)}, u32[]{:S(2)}, u32[]{:S(2)}) collective-permute-start(bf16[512,512]{1,0:T(8,128)(2,1)} %param.6), channel_id=1, source_target_pairs={{0,1},{1,2},{2,3},{3,4},{4,5},{5,6},{6,7},{7,8},{8,9},{9,10},{10,1... | collective-permute-start | bytes 1572872 | tf_op jit(solution)/shard_map/ppermute | solution.py:10
  3.2 0.7 copy-start.2
  4.0 39.1 %copy-start.3 = (f32[512]{0:T(512)S(1)}, f32[512]{0:T(512)}, u32[]{:S(2)}) copy-start(f32[512]{0:T(512)} %param.7) | copy-start | bytes 6148
  11.3 82.6 %collective-permute-start.4 = (bf16[512,512]{1,0:T(8,128)(2,1)S(1)}, bf16[512,512]{1,0:T(8,128)(2,1)S(1)}, u32[]{:S(2)}, u32[]{:S(2)}) collective-permute-start(bf16[512,512]{1,0:T(8,128)(2,1)S(1)} %collective-permute-done), channel_id=1, source_target_pairs={{0,32},{32,64},{64,96},{96,128},{128,160},{160,192},{192,224},{224... | collective-permute-start | bytes 1572872 | tf_op jit(solution)/shard_map/ppermute | solution.py:10
  22.3 18.7 %collective-permute-start.1 = (bf16[3,512]{1,0:T(4,128)(2,1)S(1)}, bf16[3,512]{1,0:T(4,128)(2,1)S(1)}, u32[]{:S(2)}, u32[]{:S(2)}) collective-permute-start(bf16[3,512]{1,0:T(4,128)(2,1)S(1)} %pad_maximum_fusion), channel_id=1, source_target_pairs={{0,1},{1,2},{2,3},{3,4},{4,5},{5,6},{6,7},{7,8},{8,9},{9,10},{10,1... | collective-permute-start | bytes 9224 | tf_op jit(solution)/shard_map/ppermute | solution.py:10
  24.2 75.1 %collective-permute-start.2 = (bf16[512,512]{1,0:T(8,128)(2,1)}, bf16[512,512]{1,0:T(8,128)(2,1)S(1)}, u32[]{:S(2)}, u32[]{:S(2)}) collective-permute-start(bf16[512,512]{1,0:T(8,128)(2,1)} %param.6), channel_id=1, source_target_pairs={{0,32},{32,64},{64,96},{96,128},{128,160},{160,192},{192,224},{224... | collective-permute-start | bytes 1572872 | tf_op jit(solution)/shard_map/ppermute | solution.py:10
  34.2 65.0 %collective-permute-start.3 = (bf16[3,512]{1,0:T(4,128)(2,1)S(1)}, bf16[3,512]{1,0:T(4,128)(2,1)S(1)}, u32[]{:S(2)}, u32[]{:S(2)}) collective-permute-start(bf16[3,512]{1,0:T(4,128)(2,1)S(1)} %pad_maximum_fusion), channel_id=1, source_target_pairs={{0,32},{32,64},{64,96},{96,128},{128,160},{160,192},{192,224},{224... | collective-permute-start | bytes 9224 | tf_op jit(solution)/shard_map/ppermute | solution.py:10
  41.0 52.9 %copy-start = (bf16[512,512]{1,0:T(8,128)(2,1)S(1)}, bf16[512,512]{1,0:T(8,128)(2,1)}, u32[]{:S(2)}) copy-start(bf16[512,512]{1,0:T(8,128)(2,1)} %param.5) | copy-start | bytes 1572868
  41.0 52.9 %collective-permute-start.5 = (bf16[3,512]{1,0:T(4,128)(2,1)S(1)}, bf16[3,512]{1,0:T(4,128)(2,1)S(1)}, u32[]{:S(2)}, u32[]{:S(2)}) collective-permute-start(bf16[3,512]{1,0:T(4,128)(2,1)S(1)} %collective-permute-done.1), channel_id=1, source_target_pairs={{0,32},{32,64},{64,96},{96,128},{128,160},{160,192},{192,224},{224... | collective-permute-start | bytes 9224 | tf_op jit(solution)/shard_map/ppermute | solution.py:10
  95.1 32.2 %collective-permute-start.7 = (f32[512,512]{1,0:T(8,128)S(1)}, f32[512,512]{1,0:T(8,128)S(1)}, u32[]{:S(2)}, u32[]{:S(2)}) collective-permute-start(f32[512,512]{1,0:T(8,128)S(1)} %fusion.11), channel_id=1, source_target_pairs={{0,992},{32,0},{64,32},{96,64},{128,96},{160,128},{192,160},{224,1... | collective-permute-start | bytes 3145736 | tf_op jit(solution)/shard_map/ppermute | solution.py:10
  100.4 182.0 %collective-permute-start.6 = (f32[512,512]{1,0:T(8,128)S(1)}, f32[512,512]{1,0:T(8,128)S(1)}, u32[]{:S(2)}, u32[]{:S(2)}) collective-permute-start(f32[512,512]{1,0:T(8,128)S(1)} %fusion.10), channel_id=1, source_target_pairs={{0,992},{32,0},{64,32},{96,64},{128,96},{160,128},{192,160},{224,1... | collective-permute-start | bytes 3145736 | tf_op jit(solution)/shard_map/ppermute | solution.py:10
  103.5 26.1 %copy-start.1 = (bf16[512,512]{1,0:T(8,128)(2,1)S(1)}, bf16[512,512]{1,0:T(8,128)(2,1)}, u32[]{:S(2)}) copy-start(bf16[512,512]{1,0:T(8,128)(2,1)} %param.6) | copy-start | bytes 1572868
  127.7 154.7 %collective-permute-start.8 = (f32[512,512]{1,0:T(8,128)S(1)}, f32[512,512]{1,0:T(8,128)S(1)}, u32[]{:S(2)}, u32[]{:S(2)}) collective-permute-start(f32[512,512]{1,0:T(8,128)S(1)} %convolution_add_fusion), channel_id=1, source_target_pairs={{0,31},{1,0},{2,1},{3,2},{4,3},{5,4},{6,5},{7,6},{8,7},{9,8},{10,9... | collective-permute-start | bytes 3145736 | tf_op jit(solution)/shard_map/ppermute | solution.py:10
where the time goes:
time: 284 us
  waiting for transfers between devices  230 us (81%)
  starting transfers between devices  41.5 us (15%)
  matrix products  9.32 us (3%)
    ppermute x9, waiting for transfers between devices, shifted(): return lax.ppermute(value, axis, pairs)  230 us
    ppermute x9, starting transfers between devices, shifted(): return lax.ppermute(value, axis, pairs)  41.5 us
  transfers between devices with their start and end apart: 9, of which 4 were waited for; matrix products, arithmetic and copies ran while one was open for 3% of the time, Pallas kernels for 0%

commit v1 on v0

v1 whole, which is shorter than its diff:
```python
import jax
import jax.numpy as jnp
from jax import lax
from jax.sharding import PartitionSpec as P

PARTS = 1


def shifted(value, axis, steps):
    count = lax.axis_size(axis)
    pairs = [(source, (source + steps) % count) for source in range(count)]
    return lax.ppermute(value, axis, pairs)


def tile_weights(images, image_stat, text_rows, text_stat, factor):
    scores = factor * lax.dot_general(
        images, text_rows, (((1,), (1,)), ((), ())), preferred_element_type=jnp.float32
    )
    return (jnp.exp(scores - image_stat[:, None]) + jnp.exp(scores - text_stat[None, :])).astype(
        jnp.bfloat16
    )


def image_side(weights, text_rows):
    return jnp.dot(weights, text_rows, preferred_element_type=jnp.float32)


def text_side(weights, images):
    return lax.dot_general(
        weights, images, (((0,), (0,)), ((), ())), preferred_element_type=jnp.float32
    )


def local(image_embeds, text_embeds, image_lse, text_lse, logit_scale):
    rows = image_embeds.shape[0]
    size = rows // PARTS
    cuts = [slice(k * size, (k + 1) * size) for k in range(PARTS)]
    far_texts = [shifted(text_embeds[cut], "outer", 1) for cut in cuts]
    far_images = [shifted(image_embeds[cut], "outer", -1) for cut in cuts]
    near_text = shifted(text_embeds, "inner", 1)
    near_image = shifted(image_embeds, "inner", -1)
    far_text_lse = shifted(text_lse, "outer", 1)
    far_image_lse = shifted(image_lse, "outer", -1)
    near_text_lse, both_text_lse = shifted(jnp.stack([text_lse, far_text_lse]), "inner", 1)
    near_image_lse, both_image_lse = shifted(jnp.stack([image_lse, far_image_lse]), "inner", -1)
    both_texts = [shifted(far, "inner", 1) for far in far_texts]
    both_images = [shifted(far, "inner", -1) for far in far_images]

    own = tile_weights(image_embeds, image_lse, text_embeds, text_lse, logit_scale)
    image_total = image_side(own, text_embeds)
    text_total = text_side(own, image_embeds)

    def add_texts(total, texts, stat):
        weights = tile_weights(image_embeds, image_lse, texts, stat, logit_scale)
        return total + image_side(weights, texts)

    def add_images(total, images, stat):
        weights = tile_weights(images, stat, text_embeds, text_lse, logit_scale)
        return total + text_side(weights, images)

    image_total = add_texts(image_total, near_text, near_text_lse)
    text_total = add_images(text_total, near_image, near_image_lse)
    for k, cut in enumerate(cuts):
        image_total = add_texts(image_total, far_texts[k], far_text_lse[cut])
        text_total = add_images(text_total, far_images[k], far_image_lse[cut])
    for k, cut in enumerate(cuts):
        image_total = add_texts(image_total, both_texts[k], both_text_lse[cut])
        text_total = add_images(text_total, both_images[k], both_image_lse[cut])
    image_grad = logit_scale * (image_total - 2.0 * text_embeds.astype(jnp.float32))
    text_grad = logit_scale * (text_total - 2.0 * image_embeds.astype(jnp.float32))
    return (image_grad, text_grad)


def solution(mesh):
    return jax.shard_map(
        local,
        mesh=mesh,
        in_specs=(
            P(("outer", "inner"), None),
            P(("outer", "inner"), None),
            P(("outer", "inner")),
            P(("outer", "inner")),
            P(),
        ),
        out_specs=(P(("outer", "inner"), None), P(("outer", "inner"), None)),
        check_vma=False,
    )
```

time: 284 us -> 142 us (0.50)
  the two profiles are of different devices: /device:TPU:118 before, /device:TPU:5 now
where the time goes in v1:
time: 142 us
  starting transfers between devices  66 us (46%)
  waiting for transfers between devices  53.4 us (38%)
  matrix products  20.3 us (14%)
  between operations  1.5 us (1%)
    ppermute x10, starting transfers between devices, shifted(): return lax.ppermute(value, axis, pairs)  66 us
    ppermute x10, waiting for transfers between devices, shifted(): return lax.ppermute(value, axis, pairs)  53.4 us
    dot_general x4, matrix products, text_side(): lax.dot_general(weights, images, (((0,), (0,)), ((), ())), preferred_elem...  9.33 us
    dot_general x4, matrix products, image_side(): return jnp.dot(weights, text_rows, preferred_element_type=jnp.float32)  9.07 us
  transfers between devices with their start and end apart: 10, of which 4 were waited for; matrix products, arithmetic and copies ran while one was open for 12% of the time, Pallas kernels for 0%

profile of v1, /device:TPU:5, one launch (start us, length us, event | category | flops | bytes accessed | tf_op | source)
XLA Modules:
  0.0 141.8 jit_solution(5571288623463581546)
XLA Ops:
  0.6 2.6 %collective-permute-start.5 = (bf16[512,512]{1,0:T(8,128)(2,1)}, bf16[512,512]{1,0:T(8,128)(2,1)}, u32[]{:S(2)}, u32[]{:S(2)}) collective-permute-start(bf16[512,512]{1,0:T(8,128)(2,1)} %param.5), channel_id=1, source_target_pairs={{0,31},{1,0},{2,1},{3,2},{4,3},{5,4},{6,5},{7,6},{8,7},{9,8},{10,9... | collective-permute-start | bytes 1572872 | tf_op jit(solution)/shard_map/ppermute | solution.py:12
  3.2 20.8 %collective-permute-start.8 = (bf16[512,512]{1,0:T(8,128)(2,1)}, bf16[512,512]{1,0:T(8,128)(2,1)}, u32[]{:S(2)}, u32[]{:S(2)}) collective-permute-start(bf16[512,512]{1,0:T(8,128)(2,1)} %param.5), channel_id=1, source_target_pairs={{0,992},{32,0},{64,32},{96,64},{128,96},{160,128},{192,160},{224,1... | collective-permute-start | bytes 1572872 | tf_op jit(solution)/shard_map/ppermute | solution.py:12
  24.0 3.4 %collective-permute-start.6 = (f32[512]{0:T(512)}, f32[512]{0:T(512)S(1)}, u32[]{:S(2)}, u32[]{:S(2)}) collective-permute-start(f32[512]{0:T(512)} %param.7), channel_id=1, source_target_pairs={{0,992},{32,0},{64,32},{96,64},{128,96},{160,128},{192,160},{224,1... | collective-permute-start | bytes 6152 | tf_op jit(solution)/shard_map/ppermute | solution.py:12
  27.4 5.8 %collective-permute-start.1 = (f32[512]{0:T(512)}, f32[512]{0:T(512)S(1)}, u32[]{:S(2)}, u32[]{:S(2)}) collective-permute-start(f32[512]{0:T(512)} %param.8), channel_id=1, source_target_pairs={{0,32},{32,64},{64,96},{96,128},{128,160},{160,192},{192,224},{224... | collective-permute-start | bytes 6152 | tf_op jit(solution)/shard_map/ppermute | solution.py:12
  33.3 3.8 %collective-permute-start = (bf16[512,512]{1,0:T(8,128)(2,1)}, bf16[512,512]{1,0:T(8,128)(2,1)}, u32[]{:S(2)}, u32[]{:S(2)}) collective-permute-start(bf16[512,512]{1,0:T(8,128)(2,1)} %param.6), channel_id=1, source_target_pairs={{0,1},{1,2},{2,3},{3,4},{4,5},{5,6},{6,7},{7,8},{8,9},{9,10},{10,1... | collective-permute-start | bytes 1572872 | tf_op jit(solution)/shard_map/ppermute | solution.py:12
  37.7 0.0 copy-start
  37.7 1.9 %add_convert_fusion.6 = bf16[512,512]{1,0:T(8,128)(2,1)S(1)} fusion(bf16[512,512]{1,0:T(8,128)(2,1)} %param.5, bf16[512,512]{1,0:T(8,128)(2,1)} %param.6, f32[512]{0:T(512)} %param.8, f32[512]{0:T(512)} %param.7, f32[]{:T(128)S(6)} %copy.7), kind=kOutput, calls=%fused_computation.23 | convolution fusion | flops 269746176 | bytes 1576964 | tf_op jit(solution)/shard_map/dot_general | solution.py:16
  39.6 0.0 copy-done
  39.7 0.0 copy-start.1
  39.7 0.5 fusion.25
  40.1 0.6 copy-done.1
  40.7 0.4 fusion.24
  41.1 0.0 copy-start.3
  41.2 28.9 %collective-permute-done.6 = f32[512]{0:T(512)S(1)} collective-permute-done((f32[512]{0:T(512)}, f32[512]{0:T(512)S(1)}, u32[]{:S(2)}, u32[]{:S(2)}) %collective-permute-start.6) | collective-permute-done | bytes 2080 | tf_op jit(solution)/shard_map/ppermute | solution.py:12
  70.0 1.9 %collective-permute-start.3 = (bf16[512,512]{1,0:T(8,128)(2,1)S(1)}, bf16[512,512]{1,0:T(8,128)(2,1)}, u32[]{:S(2)}, u32[]{:S(2)}) collective-permute-start(bf16[512,512]{1,0:T(8,128)(2,1)S(1)} %copy-done.1), channel_id=1, source_target_pairs={{0,32},{32,64},{64,96},{96,128},{128,160},{160,192},{192,224},{224... | collective-permute-start | bytes 1572872 | tf_op jit(solution)/shard_map/ppermute | solution.py:12
  72.0 0.0 copy-done.3
  72.0 0.0 copy-start.2
  72.0 0.0 collective-permute-done.1
  72.0 2.7 %collective-permute-start.7 = (f32[2,512]{1,0:T(2,128)S(1)}, f32[2,512]{1,0:T(2,128)S(1)}, u32[]{:S(2)}, u32[]{:S(2)}) collective-permute-start(f32[2,512]{1,0:T(2,128)S(1)} %pad_maximum_fusion.1), channel_id=1, source_target_pairs={{0,31},{1,0},{2,1},{3,2},{4,3},{5,4},{6,5},{7,6},{8,7},{9,8},{10,9... | collective-permute-start | bytes 12296 | tf_op jit(solution)/shard_map/ppermute | solution.py:12
  74.7 0.0 copy-done.2
  74.8 2.2 %collective-permute-done.7 = f32[2,512]{1,0:T(2,128)S(1)} collective-permute-done((f32[2,512]{1,0:T(2,128)S(1)}, f32[2,512]{1,0:T(2,128)S(1)}, u32[]{:S(2)}, u32[]{:S(2)}) %collective-permute-start.7) | collective-permute-done | bytes 4128 | tf_op jit(solution)/shard_map/ppermute | solution.py:12
  76.9 1.9 %collective-permute-start.2 = (f32[2,512]{1,0:T(2,128)S(1)}, f32[2,512]{1,0:T(2,128)S(1)}, u32[]{:S(2)}, u32[]{:S(2)}) collective-permute-start(f32[2,512]{1,0:T(2,128)S(1)} %pad_maximum_fusion), channel_id=1, source_target_pairs={{0,1},{1,2},{2,3},{3,4},{4,5},{5,6},{6,7},{7,8},{8,9},{9,10},{10,1... | collective-permute-start | bytes 12296 | tf_op jit(solution)/shard_map/ppermute | solution.py:12
  78.9 1.1 collective-permute-done.2
  80.0 0.0 collective-permute-done.8
  80.0 2.9 %collective-permute-start.9 = (bf16[512,512]{1,0:T(8,128)(2,1)}, bf16[512,512]{1,0:T(8,128)(2,1)}, u32[]{:S(2)}, u32[]{:S(2)}) collective-permute-start(bf16[512,512]{1,0:T(8,128)(2,1)} %collective-permute-done.8), channel_id=1, source_target_pairs={{0,31},{1,0},{2,1},{3,2},{4,3},{5,4},{6,5},{7,6},{8,7},{9,8},{10,9... | collective-permute-start | bytes 1572872 | tf_op jit(solution)/shard_map/ppermute | solution.py:12
  82.9 21.2 %collective-permute-done.3 = bf16[512,512]{1,0:T(8,128)(2,1)} collective-permute-done((bf16[512,512]{1,0:T(8,128)(2,1)S(1)}, bf16[512,512]{1,0:T(8,128)(2,1)}, u32[]{:S(2)}, u32[]{:S(2)}) %collective-permute-start.3) | collective-permute-done | bytes 524320 | tf_op jit(solution)/shard_map/ppermute | solution.py:12
  104.1 20.1 %collective-permute-start.4 = (bf16[512,512]{1,0:T(8,128)(2,1)}, bf16[512,512]{1,0:T(8,128)(2,1)}, u32[]{:S(2)}, u32[]{:S(2)}) collective-permute-start(bf16[512,512]{1,0:T(8,128)(2,1)} %collective-permute-done.3), channel_id=1, source_target_pairs={{0,1},{1,2},{2,3},{3,4},{4,5},{5,6},{6,7},{7,8},{8,9},{9,10},{10,1... | collective-permute-start | bytes 1572872 | tf_op jit(solution)/shard_map/ppermute | solution.py:12
  124.2 0.0 collective-permute-done.5
  124.3 3.2 %convolution_add_fusion.2 = f32[512,512]{1,0:T(8,128)} fusion(f32[512,512]{1,0:T(8,128)S(1)} %fusion.25, bf16[512,512]{1,0:T(8,128)(2,1)} %collective-permute-done.5, bf16[512,512]{1,0:T(8,128)(2,1)S(1)} %copy-done.1, f32[512]{0:T(512)S(1)} %bitcast.39, f32[512]{0:T(512)S(1)} %copy-done.2, f32[]{:T(128)S(6)} %copy.7), kind=kOutput, calls=%fused_computation.6 | convolution fusion | flops 538443776 | bytes 3149828 | tf_op jit(solution)/shard_map/dot_general | solution.py:29
  127.4 2.5 %convolution_add_fusion.1 = f32[512,512]{1,0:T(8,128)S(1)} fusion(f32[512,512]{1,0:T(8,128)} %convolution_add_fusion.2, bf16[512,512]{1,0:T(8,128)(2,1)} %collective-permute-done.8, bf16[512,512]{1,0:T(8,128)(2,1)S(1)} %copy-done.1, f32[512]{0:T(512)S(1)} %collective-permute-done.6, f32[512]{0:T(512)S(1)} %copy-done.2, f32[]{:T(128)S(6)} %copy.7), kind=kOutput, calls=%fused_computation.4 | convolution fusion | flops 538443776 | bytes 3149828 | tf_op jit(solution)/shard_map/dot_general | solution.py:29
  129.9 0.0 collective-permute-done
  130.0 3.1 %convolution_add_fusion.5 = f32[512,512]{1,0:T(8,128)} fusion(f32[512,512]{1,0:T(8,128)S(1)} %fusion.24, bf16[512,512]{1,0:T(8,128)(2,1)} %collective-permute-done, bf16[512,512]{1,0:T(8,128)(2,1)S(1)} %copy-done, f32[512]{0:T(512)S(1)} %bitcast.38, f32[512]{0:T(512)S(1)} %copy-done.3, f32[]{:T(128)S(6)} %copy.7), kind=kOutput, calls=%fused_computation.14 | convolution fusion | flops 538443776 | bytes 3149828 | tf_op jit(solution)/shard_map/dot_general | solution.py:25
  133.0 2.4 %convolution_add_fusion.4 = f32[512,512]{1,0:T(8,128)S(1)} fusion(f32[512,512]{1,0:T(8,128)} %convolution_add_fusion.5, bf16[512,512]{1,0:T(8,128)(2,1)} %collective-permute-done.3, bf16[512,512]{1,0:T(8,128)(2,1)S(1)} %copy-done, f32[512]{0:T(512)S(1)} %collective-permute-done.1, f32[512]{0:T(512)S(1)} %copy-done.3, f32[]{:T(128)S(6)} %copy.7), kind=kOutput, calls=%fused_computation.12 | convolution fusion | flops 538443776 | bytes 3149828 | tf_op jit(solution)/shard_map/dot_general | solution.py:25
  135.5 0.0 collective-permute-done.9
  135.5 3.2 %fusion.1 = f32[512,512]{1,0:T(8,128)} fusion(f32[512,512]{1,0:T(8,128)S(1)} %convolution_add_fusion.1, bf16[512,512]{1,0:T(8,128)(2,1)} %collective-permute-done.9, bf16[512,512]{1,0:T(8,128)(2,1)S(1)} %copy-done, bf16[512,512]{1,0:T(8,128)(2,1)S(1)} %copy-done.1, f32[512]{0:T(512)S(1)} %bitcast.37, f32[512]{0:T(512)S(1)} %copy-done.2, f32[]{:T(128)S(6)} %copy.7), kind=kOutput, calls=%fused_computation.2 | convolution fusion | flops 539492352 | bytes 3674116 | tf_op jit(solution)/shard_map/dot_general | solution.py:29
  138.7 0.0 collective-permute-done.4
  138.7 3.1 %fusion.3 = f32[512,512]{1,0:T(8,128)} fusion(f32[512,512]{1,0:T(8,128)S(1)} %convolution_add_fusion.4, bf16[512,512]{1,0:T(8,128)(2,1)} %collective-permute-done.4, bf16[512,512]{1,0:T(8,128)(2,1)S(1)} %copy-done.1, bf16[512,512]{1,0:T(8,128)(2,1)S(1)} %copy-done, f32[512]{0:T(512)S(1)} %bitcast.36, f32[512]{0:T(512)S(1)} %copy-done.3, f32[]{:T(128)S(6)} %copy.7), kind=kOutput, calls=%fused_computation.10 | convolution fusion | flops 539492352 | bytes 3674116 | tf_op jit(solution)/shard_map/dot_general | solution.py:25
  (4 shorter events, 0.0 us)
Async XLA Ops:
  0.6 123.6 %collective-permute-start.5 = (bf16[512,512]{1,0:T(8,128)(2,1)}, bf16[512,512]{1,0:T(8,128)(2,1)}, u32[]{:S(2)}, u32[]{:S(2)}) collective-permute-start(bf16[512,512]{1,0:T(8,128)(2,1)} %param.5), channel_id=1, source_target_pairs={{0,31},{1,0},{2,1},{3,2},{4,3},{5,4},{6,5},{7,6},{8,7},{9,8},{10,9... | collective-permute-start | bytes 1572872 | tf_op jit(solution)/shard_map/ppermute | solution.py:12
  3.2 76.8 %collective-permute-start.8 = (bf16[512,512]{1,0:T(8,128)(2,1)}, bf16[512,512]{1,0:T(8,128)(2,1)}, u32[]{:S(2)}, u32[]{:S(2)}) collective-permute-start(bf16[512,512]{1,0:T(8,128)(2,1)} %param.5), channel_id=1, source_target_pairs={{0,992},{32,0},{64,32},{96,64},{128,96},{160,128},{192,160},{224,1... | collective-permute-start | bytes 1572872 | tf_op jit(solution)/shard_map/ppermute | solution.py:12
  24.0 46.0 %collective-permute-start.6 = (f32[512]{0:T(512)}, f32[512]{0:T(512)S(1)}, u32[]{:S(2)}, u32[]{:S(2)}) collective-permute-start(f32[512]{0:T(512)} %param.7), channel_id=1, source_target_pairs={{0,992},{32,0},{64,32},{96,64},{128,96},{160,128},{192,160},{224,1... | collective-permute-start | bytes 6152 | tf_op jit(solution)/shard_map/ppermute | solution.py:12
  27.4 44.6 %collective-permute-start.1 = (f32[512]{0:T(512)}, f32[512]{0:T(512)S(1)}, u32[]{:S(2)}, u32[]{:S(2)}) collective-permute-start(f32[512]{0:T(512)} %param.8), channel_id=1, source_target_pairs={{0,32},{32,64},{64,96},{96,128},{128,160},{160,192},{192,224},{224... | collective-permute-start | bytes 6152 | tf_op jit(solution)/shard_map/ppermute | solution.py:12
  33.3 96.7 %collective-permute-start = (bf16[512,512]{1,0:T(8,128)(2,1)}, bf16[512,512]{1,0:T(8,128)(2,1)}, u32[]{:S(2)}, u32[]{:S(2)}) collective-permute-start(bf16[512,512]{1,0:T(8,128)(2,1)} %param.6), channel_id=1, source_target_pairs={{0,1},{1,2},{2,3},{3,4},{4,5},{5,6},{6,7},{7,8},{8,9},{9,10},{10,1... | collective-permute-start | bytes 1572872 | tf_op jit(solution)/shard_map/ppermute | solution.py:12
  37.7 1.9 %copy-start = (bf16[512,512]{1,0:T(8,128)(2,1)S(1)}, bf16[512,512]{1,0:T(8,128)(2,1)}, u32[]{:S(2)}) copy-start(bf16[512,512]{1,0:T(8,128)(2,1)} %param.5) | copy-start | bytes 1572868
  39.7 1.0 copy-start.1
  41.1 30.8 %copy-start.3 = (f32[512]{0:T(512)S(1)}, f32[512]{0:T(512)}, u32[]{:S(2)}) copy-start(f32[512]{0:T(512)} %param.7) | copy-start | bytes 6148
  70.0 34.1 %collective-permute-start.3 = (bf16[512,512]{1,0:T(8,128)(2,1)S(1)}, bf16[512,512]{1,0:T(8,128)(2,1)}, u32[]{:S(2)}, u32[]{:S(2)}) collective-permute-start(bf16[512,512]{1,0:T(8,128)(2,1)S(1)} %copy-done.1), channel_id=1, source_target_pairs={{0,32},{32,64},{64,96},{96,128},{128,160},{160,192},{192,224},{224... | collective-permute-start | bytes 1572872 | tf_op jit(solution)/shard_map/ppermute | solution.py:12
  72.0 2.8 %copy-start.2 = (f32[512]{0:T(512)S(1)}, f32[512]{0:T(512)}, u32[]{:S(2)}) copy-start(f32[512]{0:T(512)} %param.8) | copy-start | bytes 6148
  72.0 4.9 %collective-permute-start.7 = (f32[2,512]{1,0:T(2,128)S(1)}, f32[2,512]{1,0:T(2,128)S(1)}, u32[]{:S(2)}, u32[]{:S(2)}) collective-permute-start(f32[2,512]{1,0:T(2,128)S(1)} %pad_maximum_fusion.1), channel_id=1, source_target_pairs={{0,31},{1,0},{2,1},{3,2},{4,3},{5,4},{6,5},{7,6},{8,7},{9,8},{10,9... | collective-permute-start | bytes 12296 | tf_op jit(solution)/shard_map/ppermute | solution.py:12
  76.9 3.0 %collective-permute-start.2 = (f32[2,512]{1,0:T(2,128)S(1)}, f32[2,512]{1,0:T(2,128)S(1)}, u32[]{:S(2)}, u32[]{:S(2)}) collective-permute-start(f32[2,512]{1,0:T(2,128)S(1)} %pad_maximum_fusion), channel_id=1, source_target_pairs={{0,1},{1,2},{2,3},{3,4},{4,5},{5,6},{6,7},{7,8},{8,9},{9,10},{10,1... | collective-permute-start | bytes 12296 | tf_op jit(solution)/shard_map/ppermute | solution.py:12
  80.0 55.5 %collective-permute-start.9 = (bf16[512,512]{1,0:T(8,128)(2,1)}, bf16[512,512]{1,0:T(8,128)(2,1)}, u32[]{:S(2)}, u32[]{:S(2)}) collective-permute-start(bf16[512,512]{1,0:T(8,128)(2,1)} %collective-permute-done.8), channel_id=1, source_target_pairs={{0,31},{1,0},{2,1},{3,2},{4,3},{5,4},{6,5},{7,6},{8,7},{9,8},{10,9... | collective-permute-start | bytes 1572872 | tf_op jit(solution)/shard_map/ppermute | solution.py:12
  104.1 34.6 %collective-permute-start.4 = (bf16[512,512]{1,0:T(8,128)(2,1)}, bf16[512,512]{1,0:T(8,128)(2,1)}, u32[]{:S(2)}, u32[]{:S(2)}) collective-permute-start(bf16[512,512]{1,0:T(8,128)(2,1)} %collective-permute-done.3), channel_id=1, source_target_pairs={{0,1},{1,2},{2,3},{3,4},{4,5},{5,6},{6,7},{7,8},{8,9},{9,10},{10,1... | collective-permute-start | bytes 1572872 | tf_op jit(solution)/shard_map/ppermute | solution.py:12

commit v2 on v1

v2 whole, which is shorter than its diff:
```python
import jax
import jax.numpy as jnp
from jax import lax
from jax.experimental import pallas as pl
from jax.experimental.pallas import tpu as pltpu
from jax.sharding import PartitionSpec as P

STAT_ROWS = 16
BLOCKS = 2
VMEM_BYTES = 16 * 1024 * 1024
PACK_VMEM_BYTES = 60 * 1024 * 1024
ON_IMAGES = (2**29, 2**30, 2**29)
ON_TEXTS = (2**29, 2**30, 2**29)


def shifted(value, axis, steps):
    count = lax.axis_size(axis)
    pairs = [(source, (source + steps) % count) for source in range(count)]
    return lax.ppermute(value, axis, pairs)


def pack_kernel(text_ref, text_stat_ref, image_ref, image_stat_ref, text_out, image_out, sems):
    rows = text_ref.shape[0]
    sides = ((text_ref, text_stat_ref, text_out), (image_ref, image_stat_ref, image_out))
    moves = [
        pltpu.make_async_copy(rows_ref, out.at[pl.ds(0, rows), :], sems.at[k])
        for k, (rows_ref, _, out) in enumerate(sides)
    ]
    for copy in moves:
        copy.start()
    for _, stat_ref, out in sides:
        stat = stat_ref[...]
        upper = stat.astype(jnp.bfloat16).astype(jnp.float32)
        rest = stat - upper
        middle = rest.astype(jnp.bfloat16).astype(jnp.float32)
        lower = rest - middle
        zeros = jnp.zeros((STAT_ROWS - 3, stat.shape[1]), jnp.float32)
        out[pl.ds(rows, STAT_ROWS), :] = jnp.concatenate(
            [upper, middle, lower, zeros], axis=0
        ).astype(jnp.bfloat16)
    for copy in moves:
        copy.wait()


def pack(text, text_stat, image, image_stat):
    rows, width = text.shape
    packed = jax.ShapeDtypeStruct((rows + STAT_ROWS, width), jnp.bfloat16)
    hbm = pl.BlockSpec(memory_space=pltpu.HBM)
    vmem = pl.BlockSpec(memory_space=pltpu.VMEM)
    return pl.pallas_call(
        pack_kernel,
        in_specs=[hbm, vmem, hbm, vmem],
        out_specs=(vmem, vmem),
        out_shape=(packed, packed),
        scratch_shapes=[pltpu.SemaphoreType.DMA((2,))],
        compiler_params=pltpu.CompilerParams(vmem_limit_bytes=PACK_VMEM_BYTES),
    )(text, text_stat.reshape(1, rows), image, image_stat.reshape(1, rows))


def tile_term(factor, own, own_stat, packed_ref):
    rows = packed_ref.shape[0] - STAT_ROWS
    other = packed_ref[pl.ds(0, rows), :]
    pieces = packed_ref[pl.ds(rows, STAT_ROWS), :].astype(jnp.float32)
    other_stat = pieces[0:1, :] + (pieces[1:2, :] + pieces[2:3, :])
    scores = factor * lax.dot_general(
        own, other, (((1,), (1,)), ((), ())), preferred_element_type=jnp.float32
    )
    weights = (jnp.exp(scores - own_stat) + jnp.exp(scores - other_stat)).astype(jnp.bfloat16)
    return jnp.dot(weights, other, preferred_element_type=jnp.float32)


def first_kernel(factor_ref, own_ref, stat_ref, same_ref, pair_ref, out_ref):
    term = tile_term(factor_ref[0, 0], own_ref[...], stat_ref[...], same_ref)
    out_ref[...] = term - 2.0 * pair_ref[...].astype(jnp.float32)


def middle_kernel(factor_ref, own_ref, stat_ref, near_ref, far_ref, total_ref, out_ref):
    factor = factor_ref[0, 0]
    own, stat = own_ref[...], stat_ref[...]
    total = total_ref[...] + tile_term(factor, own, stat, near_ref)
    out_ref[...] = total + tile_term(factor, own, stat, far_ref)


def last_kernel(factor_ref, own_ref, stat_ref, both_ref, total_ref, out_ref):
    factor = factor_ref[0, 0]
    out_ref[...] = factor * (
        total_ref[...] + tile_term(factor, own_ref[...], stat_ref[...], both_ref)
    )


def call(kernel, flops, factor, own, stat, *arrays):
    rows, width = own.shape
    size = rows // BLOCKS
    blocked = pl.BlockSpec((size, width), lambda k: (k, 0))
    whole = pl.BlockSpec((rows + STAT_ROWS, width), lambda k: (0, 0))
    specs = [whole if a.shape[0] != rows else blocked for a in arrays]
    return pl.pallas_call(
        kernel,
        grid=(BLOCKS,),
        in_specs=[
            pl.BlockSpec(memory_space=pltpu.SMEM),
            blocked,
            pl.BlockSpec((size, 1), lambda k: (k, 0)),
            *specs,
        ],
        out_specs=blocked,
        out_shape=jax.ShapeDtypeStruct((rows, width), jnp.float32),
        compiler_params=pltpu.CompilerParams(vmem_limit_bytes=VMEM_BYTES),
        cost_estimate=pl.CostEstimate(
            flops=flops, bytes_accessed=flops // 1000, transcendentals=0
        ),
    )(factor, own, stat, *arrays)


def local(image_embeds, text_embeds, image_lse, text_lse, logit_scale):
    rows = image_embeds.shape[0]
    factor = logit_scale.reshape(1, 1)
    text, image = pack(text_embeds, text_lse, image_embeds, image_lse)
    far_text = shifted(text, "outer", 1)
    far_image = shifted(image, "outer", -1)
    near_text = shifted(text, "inner", 1)
    near_image = shifted(image, "inner", -1)

    on_images = (factor, image_embeds, image_lse.reshape(rows, 1))
    on_texts = (factor, text_embeds, text_lse.reshape(rows, 1))
    image_total = call(first_kernel, ON_IMAGES[0], *on_images, text, text_embeds)
    text_total = call(first_kernel, ON_TEXTS[0], *on_texts, image, image_embeds)
    far_text, image_total = lax.optimization_barrier((far_text, image_total))
    far_image, text_total = lax.optimization_barrier((far_image, text_total))
    both_text = shifted(far_text, "inner", 1)
    both_image = shifted(far_image, "inner", -1)
    image_total = call(middle_kernel, ON_IMAGES[1], *on_images, near_text, far_text, image_total)
    text_total = call(middle_kernel, ON_TEXTS[1], *on_texts, near_image, far_image, text_total)
    image_grad = call(last_kernel, ON_IMAGES[2], *on_images, both_text, image_total)
    both_image, image_grad = lax.optimization_barrier((both_image, image_grad))
    text_grad = call(last_kernel, ON_TEXTS[2], *on_texts, both_image, text_total)
    return (image_grad, text_grad)


def solution(mesh):
    return jax.shard_map(
        local,
        mesh=mesh,
        in_specs=(
            P(("outer", "inner"), None),
            P(("outer", "inner"), None),
            P(("outer", "inner")),
            P(("outer", "inner")),
            P(),
        ),
        out_specs=(P(("outer", "inner"), None), P(("outer", "inner"), None)),
        check_vma=False,
    )
```

time: 142 us -> 93.1 us (0.66)
  the two profiles are of different devices: /device:TPU:5 before, /device:TPU:175 now
where the time goes in v2:
time: 93.1 us; the launch traced here: 92.7 us
  starting transfers between devices  42.6 us (46%)
  waiting for transfers between devices  32.3 us (35%)
  Pallas kernels  14.8 us (16%)
  between operations  1.49 us (2%)
  local copies, waits for them, and re-layouts  1.35 us (1%)
    ppermute x6, starting transfers between devices, shifted(): return lax.ppermute(value, axis, pairs)  42.6 us
    ppermute x6, waiting for transfers between devices, shifted(): return lax.ppermute(value, axis, pairs)  32.3 us
    pallas_call x6, Pallas kernels, call(): pl.pallas_call(kernel, grid=(BLOCKS,), in_specs=[pl.BlockSpec(memory_spac...  11.9 us
    pallas_call x1, Pallas kernels, pack(): pl.pallas_call(pack_kernel, in_specs=[hbm, vmem, hbm, vmem], out_specs=(v...  2.95 us
  transfers between devices with their start and end apart: 6, of which 3 were waited for; matrix products, arithmetic and copies ran while one was open for 0% of the time, Pallas kernels for 11%

profile of v2, /device:TPU:175, one launch (start us, length us, event | category | flops | bytes accessed | tf_op | source)
XLA Modules:
  0.0 92.7 jit_solution(14388745022899475919)
XLA Ops:
  0.6 0.0 copy-start.4
  0.6 0.0 copy-start.5
  0.7 0.0 copy-start.1
  0.7 3.0 %shard_map.68 = (bf16[528,512]{1,0:T(8,128)(2,1)}, bf16[528,512]{1,0:T(8,128)(2,1)}) custom-call(bf16[512,512]{1,0:T(8,128)(2,1)} %own_ref.11, f32[1,512]{1,0:T(1,128)} %bitcast.13, bf16[512,512]{1,0:T(8,128)(2,1)} %own_ref.9, f32[1,512]{1,0:T(1,128)} %bitcast.11), custom_call_target="tpu_custom_call" | custom-call | tf_op jit(solution)/shard_map/pallas_call | solution.py:50
  3.6 0.0 copy-start
  3.6 10.8 %collective-permute-start.2 = (bf16[528,512]{1,0:T(8,128)(2,1)}, bf16[528,512]{1,0:T(8,128)(2,1)S(1)}, u32[]{:S(2)}, u32[]{:S(2)}) collective-permute-start(bf16[528,512]{1,0:T(8,128)(2,1)} %get-tuple-element.12.same_ref), channel_id=1, source_target_pairs={{0,32},{32,64},{64,96},{96,128},{128,160},{160,192},{192,224},{224... | collective-permute-start | bytes 1622024 | tf_op jit(solution)/shard_map/ppermute | solution.py:19
  14.4 8.2 %collective-permute-start = (bf16[528,512]{1,0:T(8,128)(2,1)}, bf16[528,512]{1,0:T(8,128)(2,1)S(1)}, u32[]{:S(2)}, u32[]{:S(2)}) collective-permute-start(bf16[528,512]{1,0:T(8,128)(2,1)} %get-tuple-element.10.same_ref), channel_id=1, source_target_pairs={{0,992},{32,0},{64,32},{96,64},{128,96},{160,128},{192,160},{224,1... | collective-permute-start | bytes 1622024 | tf_op jit(solution)/shard_map/ppermute | solution.py:19
  22.6 3.9 %collective-permute-start.4 = (bf16[528,512]{1,0:T(8,128)(2,1)}, bf16[528,512]{1,0:T(8,128)(2,1)}, u32[]{:S(2)}, u32[]{:S(2)}) collective-permute-start(bf16[528,512]{1,0:T(8,128)(2,1)} %get-tuple-element.12.same_ref), channel_id=1, source_target_pairs={{0,1},{1,2},{2,3},{3,4},{4,5},{5,6},{6,7},{7,8},{8,9},{9,10},{10,1... | collective-permute-start | bytes 1622024 | tf_op jit(solution)/shard_map/ppermute | solution.py:19
  26.5 1.9 %collective-permute-start.5 = (bf16[528,512]{1,0:T(8,128)(2,1)}, bf16[528,512]{1,0:T(8,128)(2,1)S(1)}, u32[]{:S(2)}, u32[]{:S(2)}) collective-permute-start(bf16[528,512]{1,0:T(8,128)(2,1)} %get-tuple-element.10.same_ref), channel_id=1, source_target_pairs={{0,31},{1,0},{2,1},{3,2},{4,3},{5,4},{6,5},{7,6},{8,7},{9,8},{10,9... | collective-permute-start | bytes 1622024 | tf_op jit(solution)/shard_map/ppermute | solution.py:19
  29.0 0.0 copy-done.4
  29.0 0.1 copy.10.stat_ref
  29.2 0.0 copy-done.5
  29.2 0.1 copy.7.stat_ref
  29.4 0.0 copy-done.1
  29.4 0.0 copy-done
  29.4 0.0 copy-start.3
  29.4 1.0 %copy-done.3 = bf16[528,512]{1,0:T(8,128)(2,1)S(1)} copy-done((bf16[528,512]{1,0:T(8,128)(2,1)S(1)}, bf16[528,512]{1,0:T(8,128)(2,1)}, u32[]{:S(2)}) %copy-start.3) | copy-done | bytes 540696
  30.4 0.0 copy-start.2
  30.4 1.2 %shard_map.70.total_ref = f32[512,512]{1,0:T(8,128)S(1)} custom-call(f32[1,1]{1,0:T(1,128)} %bitcast.6.factor_ref, bf16[512,512]{1,0:T(8,128)(2,1)S(1)} %copy-done, f32[512,1]{1,0:T(8,128)S(1)} %copy.10.stat_ref, bf16[528,512]{1,0:T(8,128)(2,1)S(1)} %copy-done.3, bf16[512,512]{1,0:T(8,128)(2,1)S(1)} %copy-done.1), custom_call_target="tpu_custom_call" | custom-call | flops 536870912 | bytes 536870 | tf_op jit(solution)/shard_map/pallas_call | solution.py:97
  31.7 25.6 %collective-permute-done.2.far_ref = bf16[528,512]{1,0:T(8,128)(2,1)S(1)} collective-permute-done((bf16[528,512]{1,0:T(8,128)(2,1)}, bf16[528,512]{1,0:T(8,128)(2,1)S(1)}, u32[]{:S(2)}, u32[]{:S(2)}) %collective-permute-start.2) | collective-permute-done | bytes 540704 | tf_op jit(solution)/shard_map/ppermute | solution.py:19
  57.3 14.5 %collective-permute-start.3 = (bf16[528,512]{1,0:T(8,128)(2,1)S(1)}, bf16[528,512]{1,0:T(8,128)(2,1)S(1)}, u32[]{:S(2)}, u32[]{:S(2)}) collective-permute-start(bf16[528,512]{1,0:T(8,128)(2,1)S(1)} %collective-permute-done.2.far_ref), channel_id=1, source_target_pairs={{0,1},{1,2},{2,3},{3,4},{4,5},{5,6},{6,7},{7,8},{8,9},{9,10},{10,1... | collective-permute-start | bytes 1622024 | tf_op jit(solution)/shard_map/ppermute | solution.py:19
  71.8 0.0 copy-done.2
  71.8 1.3 %shard_map.69.total_ref = f32[512,512]{1,0:T(8,128)S(1)} custom-call(f32[1,1]{1,0:T(1,128)} %bitcast.5.factor_ref, bf16[512,512]{1,0:T(8,128)(2,1)S(1)} %copy-done.1, f32[512,1]{1,0:T(8,128)S(1)} %copy.7.stat_ref, bf16[528,512]{1,0:T(8,128)(2,1)S(1)} %copy-done.2, bf16[512,512]{1,0:T(8,128)(2,1)S(1)} %copy-done), custom_call_target="tpu_custom_call" | custom-call | flops 536870912 | bytes 536870 | tf_op jit(solution)/shard_map/pallas_call | solution.py:97
  73.1 4.8 %collective-permute-done.far_ref = bf16[528,512]{1,0:T(8,128)(2,1)S(1)} collective-permute-done((bf16[528,512]{1,0:T(8,128)(2,1)}, bf16[528,512]{1,0:T(8,128)(2,1)S(1)}, u32[]{:S(2)}, u32[]{:S(2)}) %collective-permute-start) | collective-permute-done | bytes 540704 | tf_op jit(solution)/shard_map/ppermute | solution.py:19
  77.9 3.4 %collective-permute-start.1 = (bf16[528,512]{1,0:T(8,128)(2,1)S(1)}, bf16[528,512]{1,0:T(8,128)(2,1)S(1)}, u32[]{:S(2)}, u32[]{:S(2)}) collective-permute-start(bf16[528,512]{1,0:T(8,128)(2,1)S(1)} %collective-permute-done.far_ref), channel_id=1, source_target_pairs={{0,31},{1,0},{2,1},{3,2},{4,3},{5,4},{6,5},{7,6},{8,7},{9,8},{10,9... | collective-permute-start | bytes 1622024 | tf_op jit(solution)/shard_map/ppermute | solution.py:19
  81.3 0.0 collective-permute-done.4.near_ref
  81.3 3.1 %shard_map.71.total_ref = f32[512,512]{1,0:T(8,128)S(1)} custom-call(f32[1,1]{1,0:T(1,128)} %bitcast.7.factor_ref, bf16[512,512]{1,0:T(8,128)(2,1)S(1)} %copy-done, f32[512,1]{1,0:T(8,128)S(1)} %copy.10.stat_ref, bf16[528,512]{1,0:T(8,128)(2,1)} %collective-permute-done.4.near_ref, bf16[528,512]{1,0:T(8,128)(2,1)S(1)} %collective-permute-done.2.far_ref, ...), custom_call_target="tpu_custom_call" | custom-call | flops 1073741824 | bytes 1073741 | tf_op jit(solution)/shard_map/pallas_call | solution.py:97
  84.4 0.0 collective-permute-done.5.near_ref
  84.5 2.1 %shard_map.73.total_ref = f32[512,512]{1,0:T(8,128)S(1)} custom-call(f32[1,1]{1,0:T(1,128)} %bitcast.9.factor_ref, bf16[512,512]{1,0:T(8,128)(2,1)S(1)} %copy-done.1, f32[512,1]{1,0:T(8,128)S(1)} %copy.7.stat_ref, bf16[528,512]{1,0:T(8,128)(2,1)S(1)} %collective-permute-done.5.near_ref, bf16[528,512]{1,0:T(8,128)(2,1)S(1)} %collective-permute-done.far_ref, ...), custom_call_target="tpu_custom_call" | custom-call | flops 1073741824 | bytes 1073741 | tf_op jit(solution)/shard_map/pallas_call | solution.py:97
  86.6 0.0 collective-permute-done.3.both_ref
  86.6 2.1 %shard_map.72 = f32[512,512]{1,0:T(8,128)} custom-call(f32[1,1]{1,0:T(1,128)} %bitcast.8.factor_ref, bf16[512,512]{1,0:T(8,128)(2,1)S(1)} %copy-done, f32[512,1]{1,0:T(8,128)S(1)} %copy.10.stat_ref, bf16[528,512]{1,0:T(8,128)(2,1)S(1)} %collective-permute-done.3.both_ref, f32[512,512]{1,0:T(8,128)S(1)} %shard_map.71.total_ref), custom_call_target="tpu_custom_call" | custom-call | flops 536870912 | bytes 536870 | tf_op jit(solution)/shard_map/pallas_call | solution.py:97
  88.7 2.0 %collective-permute-done.1.both_ref = bf16[528,512]{1,0:T(8,128)(2,1)S(1)} collective-permute-done((bf16[528,512]{1,0:T(8,128)(2,1)S(1)}, bf16[528,512]{1,0:T(8,128)(2,1)S(1)}, u32[]{:S(2)}, u32[]{:S(2)}) %collective-permute-start.1) | collective-permute-done | bytes 540704 | tf_op jit(solution)/shard_map/ppermute | solution.py:19
  90.6 2.1 %shard_map.74 = f32[512,512]{1,0:T(8,128)} custom-call(f32[1,1]{1,0:T(1,128)} %bitcast.10.factor_ref, bf16[512,512]{1,0:T(8,128)(2,1)S(1)} %copy-done.1, f32[512,1]{1,0:T(8,128)S(1)} %copy.7.stat_ref, bf16[528,512]{1,0:T(8,128)(2,1)S(1)} %collective-permute-done.1.both_ref, f32[512,512]{1,0:T(8,128)S(1)} %shard_map.73.total_ref), custom_call_target="tpu_custom_call" | custom-call | flops 536870912 | bytes 536870 | tf_op jit(solution)/shard_map/pallas_call | solution.py:97
Async XLA Ops:
  0.6 28.4 %copy-start.4 = (f32[512]{0:T(512)S(1)}, f32[512]{0:T(512)}, u32[]{:S(2)}) copy-start(f32[512]{0:T(512)} %param.7) | copy-start | bytes 6148
  0.6 28.6 %copy-start.5 = (f32[512]{0:T(512)S(1)}, f32[512]{0:T(512)}, u32[]{:S(2)}) copy-start(f32[512]{0:T(512)} %param.8) | copy-start | bytes 6148
  0.7 28.7 %copy-start.1 = (bf16[512,512]{1,0:T(8,128)(2,1)S(1)}, bf16[512,512]{1,0:T(8,128)(2,1)}, u32[]{:S(2)}) copy-start(bf16[512,512]{1,0:T(8,128)(2,1)} %own_ref.11) | copy-start | bytes 1572868
  3.6 25.8 %copy-start = (bf16[512,512]{1,0:T(8,128)(2,1)S(1)}, bf16[512,512]{1,0:T(8,128)(2,1)}, u32[]{:S(2)}) copy-start(bf16[512,512]{1,0:T(8,128)(2,1)} %own_ref.9) | copy-start | bytes 1572868
  3.6 53.7 %collective-permute-start.2 = (bf16[528,512]{1,0:T(8,128)(2,1)}, bf16[528,512]{1,0:T(8,128)(2,1)S(1)}, u32[]{:S(2)}, u32[]{:S(2)}) collective-permute-start(bf16[528,512]{1,0:T(8,128)(2,1)} %get-tuple-element.12.same_ref), channel_id=1, source_target_pairs={{0,32},{32,64},{64,96},{96,128},{128,160},{160,192},{192,224},{224... | collective-permute-start | bytes 1622024 | tf_op jit(solution)/shard_map/ppermute | solution.py:19
  14.4 63.4 %collective-permute-start = (bf16[528,512]{1,0:T(8,128)(2,1)}, bf16[528,512]{1,0:T(8,128)(2,1)S(1)}, u32[]{:S(2)}, u32[]{:S(2)}) collective-permute-start(bf16[528,512]{1,0:T(8,128)(2,1)} %get-tuple-element.10.same_ref), channel_id=1, source_target_pairs={{0,992},{32,0},{64,32},{96,64},{128,96},{160,128},{192,160},{224,1... | collective-permute-start | bytes 1622024 | tf_op jit(solution)/shard_map/ppermute | solution.py:19
  22.6 58.7 %collective-permute-start.4 = (bf16[528,512]{1,0:T(8,128)(2,1)}, bf16[528,512]{1,0:T(8,128)(2,1)}, u32[]{:S(2)}, u32[]{:S(2)}) collective-permute-start(bf16[528,512]{1,0:T(8,128)(2,1)} %get-tuple-element.12.same_ref), channel_id=1, source_target_pairs={{0,1},{1,2},{2,3},{3,4},{4,5},{5,6},{6,7},{7,8},{8,9},{9,10},{10,1... | collective-permute-start | bytes 1622024 | tf_op jit(solution)/shard_map/ppermute | solution.py:19
  26.5 58.0 %collective-permute-start.5 = (bf16[528,512]{1,0:T(8,128)(2,1)}, bf16[528,512]{1,0:T(8,128)(2,1)S(1)}, u32[]{:S(2)}, u32[]{:S(2)}) collective-permute-start(bf16[528,512]{1,0:T(8,128)(2,1)} %get-tuple-element.10.same_ref), channel_id=1, source_target_pairs={{0,31},{1,0},{2,1},{3,2},{4,3},{5,4},{6,5},{7,6},{8,7},{9,8},{10,9... | collective-permute-start | bytes 1622024 | tf_op jit(solution)/shard_map/ppermute | solution.py:19
  29.4 1.1 %copy-start.3 = (bf16[528,512]{1,0:T(8,128)(2,1)S(1)}, bf16[528,512]{1,0:T(8,128)(2,1)}, u32[]{:S(2)}) copy-start(bf16[528,512]{1,0:T(8,128)(2,1)} %get-tuple-element.12.same_ref) | copy-start | bytes 1622020
  30.4 41.4 %copy-start.2 = (bf16[528,512]{1,0:T(8,128)(2,1)S(1)}, bf16[528,512]{1,0:T(8,128)(2,1)}, u32[]{:S(2)}) copy-start(bf16[528,512]{1,0:T(8,128)(2,1)} %get-tuple-element.10.same_ref) | copy-start | bytes 1622020
  57.3 29.3 %collective-permute-start.3 = (bf16[528,512]{1,0:T(8,128)(2,1)S(1)}, bf16[528,512]{1,0:T(8,128)(2,1)S(1)}, u32[]{:S(2)}, u32[]{:S(2)}) collective-permute-start(bf16[528,512]{1,0:T(8,128)(2,1)S(1)} %collective-permute-done.2.far_ref), channel_id=1, source_target_pairs={{0,1},{1,2},{2,3},{3,4},{4,5},{5,6},{6,7},{7,8},{8,9},{9,10},{10,1... | collective-permute-start | bytes 1622024 | tf_op jit(solution)/shard_map/ppermute | solution.py:19
  77.9 12.8 %collective-permute-start.1 = (bf16[528,512]{1,0:T(8,128)(2,1)S(1)}, bf16[528,512]{1,0:T(8,128)(2,1)S(1)}, u32[]{:S(2)}, u32[]{:S(2)}) collective-permute-start(bf16[528,512]{1,0:T(8,128)(2,1)S(1)} %collective-permute-done.far_ref), channel_id=1, source_target_pairs={{0,31},{1,0},{2,1},{3,2},{4,3},{5,4},{6,5},{7,6},{8,7},{9,8},{10,9... | collective-permute-start | bytes 1622024 | tf_op jit(solution)/shard_map/ppermute | solution.py:19

commit v3 on v2

v3 whole, which is shorter than its diff:
```python
import jax
import jax.numpy as jnp
from jax import lax
from jax.experimental import pallas as pl
from jax.experimental.pallas import tpu as pltpu
from jax.sharding import PartitionSpec as P

STAT_ROWS = 16
BLOCKS = 4
VMEM_BYTES = 16 * 1024 * 1024
PACK_VMEM_BYTES = 8 * 1024 * 1024
COSTS = (2**29, 2**30, 2**29)


def shifted(value, axis, steps):
    count = lax.axis_size(axis)
    pairs = [(source, (source + steps) % count) for source in range(count)]
    return lax.ppermute(value, axis, pairs)


def pack_kernel(rows_ref, stat_ref, out, sem):
    rows = rows_ref.shape[0]
    copy = pltpu.make_async_copy(rows_ref, out.at[pl.ds(0, rows), :], sem)
    copy.start()
    stat = stat_ref[...]
    upper = stat.astype(jnp.bfloat16).astype(jnp.float32)
    rest = stat - upper
    middle = rest.astype(jnp.bfloat16).astype(jnp.float32)
    lower = rest - middle
    zeros = jnp.zeros((STAT_ROWS - 3, stat.shape[1]), jnp.float32)
    out[pl.ds(rows, STAT_ROWS), :] = jnp.concatenate(
        [upper, middle, lower, zeros], axis=0
    ).astype(jnp.bfloat16)
    copy.wait()


def pack(block, stat):
    rows, width = block.shape
    vmem = pl.BlockSpec(memory_space=pltpu.VMEM)
    return pl.pallas_call(
        pack_kernel,
        in_specs=[pl.BlockSpec(memory_space=pltpu.HBM), vmem],
        out_specs=vmem,
        out_shape=jax.ShapeDtypeStruct((rows + STAT_ROWS, width), jnp.bfloat16),
        scratch_shapes=[pltpu.SemaphoreType.DMA],
        compiler_params=pltpu.CompilerParams(vmem_limit_bytes=PACK_VMEM_BYTES),
    )(block, stat.reshape(1, rows))


def blocks(packed_ref):
    rows = packed_ref.shape[0] - STAT_ROWS
    size = rows // BLOCKS
    return [pl.ds(k * size, size) for k in range(BLOCKS)]


def tile_term(factor, own, own_stat, packed_ref):
    rows = packed_ref.shape[0] - STAT_ROWS
    other = packed_ref[pl.ds(0, rows), :]
    pieces = packed_ref[pl.ds(rows, STAT_ROWS), :].astype(jnp.float32)
    other_stat = pieces[0:1, :] + (pieces[1:2, :] + pieces[2:3, :])
    scores = factor * lax.dot_general(
        own, other, (((1,), (1,)), ((), ())), preferred_element_type=jnp.float32
    )
    weights = (jnp.exp(scores - own_stat) + jnp.exp(scores - other_stat)).astype(jnp.bfloat16)
    return jnp.dot(weights, other, preferred_element_type=jnp.float32)


def first_kernel(factor_ref, own_ref, stat_ref, pair_ref, out_ref):
    factor = factor_ref[0, 0]
    for cut in blocks(own_ref):
        term = tile_term(factor, own_ref[cut, :], stat_ref[cut, :], pair_ref)
        out_ref[cut, :] = term - 2.0 * pair_ref[cut, :].astype(jnp.float32)


def middle_kernel(factor_ref, own_ref, stat_ref, near_ref, far_ref, total_ref, out_ref):
    factor = factor_ref[0, 0]
    for cut in blocks(own_ref):
        own, stat = own_ref[cut, :], stat_ref[cut, :]
        total = total_ref[cut, :] + tile_term(factor, own, stat, near_ref)
        out_ref[cut, :] = total + tile_term(factor, own, stat, far_ref)


def last_kernel(factor_ref, own_ref, stat_ref, both_ref, total_ref, out_ref, done, sems):
    factor = factor_ref[0, 0]
    copies = []
    for k, cut in enumerate(blocks(own_ref)):
        term = tile_term(factor, own_ref[cut, :], stat_ref[cut, :], both_ref)
        done[cut, :] = factor * (total_ref[cut, :] + term)
        copies.append(pltpu.make_async_copy(done.at[cut, :], out_ref.at[cut, :], sems.at[k]))
        copies[k].start()
    for copy in copies:
        copy.wait()


def call(kernel, flops, factor, own, stat, *arrays):
    rows, width = stat.shape[0], own.shape[1]
    vmem = pl.BlockSpec(memory_space=pltpu.VMEM)
    last = kernel is last_kernel
    scratch = [pltpu.VMEM((rows, width), jnp.float32), pltpu.SemaphoreType.DMA((BLOCKS,))]
    return pl.pallas_call(
        kernel,
        in_specs=[pl.BlockSpec(memory_space=pltpu.SMEM)] + [vmem] * (2 + len(arrays)),
        out_specs=pl.BlockSpec(memory_space=pltpu.HBM) if last else vmem,
        out_shape=jax.ShapeDtypeStruct((rows, width), jnp.float32),
        scratch_shapes=scratch if last else [],
        compiler_params=pltpu.CompilerParams(vmem_limit_bytes=VMEM_BYTES),
        cost_estimate=pl.CostEstimate(
            flops=flops, bytes_accessed=flops // 1000, transcendentals=0
        ),
    )(factor, own, stat, *arrays)


def local(image_embeds, text_embeds, image_lse, text_lse, logit_scale):
    rows = image_embeds.shape[0]
    factor = logit_scale.reshape(1, 1)
    text = pack(text_embeds, text_lse)
    image = pack(image_embeds, image_lse)
    far_text = shifted(text, "outer", 1)
    far_image = shifted(image, "outer", -1)
    near_text = shifted(text, "inner", 1)
    near_image = shifted(image, "inner", -1)

    on_images = (factor, image, image_lse.reshape(rows, 1))
    on_texts = (factor, text, text_lse.reshape(rows, 1))
    image_total = call(first_kernel, COSTS[0], *on_images, text)
    text_total = call(first_kernel, COSTS[0], *on_texts, image)
    far_text, image_total = lax.optimization_barrier((far_text, image_total))
    far_image, text_total = lax.optimization_barrier((far_image, text_total))
    both_text = shifted(far_text, "inner", 1)
    both_image = shifted(far_image, "inner", -1)
    image_total = call(middle_kernel, COSTS[1], *on_images, near_text, far_text, image_total)
    text_total = call(middle_kernel, COSTS[1], *on_texts, near_image, far_image, text_total)
    image_grad = call(last_kernel, COSTS[2], *on_images, both_text, image_total)
    both_image, image_grad = lax.optimization_barrier((both_image, image_grad))
    text_grad = call(last_kernel, COSTS[2], *on_texts, both_image, text_total)
    return (image_grad, text_grad)


def solution(mesh):
    return jax.shard_map(
        local,
        mesh=mesh,
        in_specs=(
            P(("outer", "inner"), None),
            P(("outer", "inner"), None),
            P(("outer", "inner")),
            P(("outer", "inner")),
            P(),
        ),
        out_specs=(P(("outer", "inner"), None), P(("outer", "inner"), None)),
        check_vma=False,
    )
```

time: 93.1 us -> 92.6 us (level)
  the two profiles are of different devices: /device:TPU:175 before, /device:TPU:183 now
where the time goes in v3:
time: 92.6 us; the launch traced here: 92.2 us
  starting transfers between devices  42.3 us (46%)
  waiting for transfers between devices  30.8 us (33%)
  Pallas kernels  15.6 us (17%)
  local copies, waits for them, and re-layouts  2.02 us (2%)
  between operations  1.47 us (2%)
    ppermute x6, starting transfers between devices, shifted(): return lax.ppermute(value, axis, pairs)  42.3 us
    ppermute x6, waiting for transfers between devices, shifted(): return lax.ppermute(value, axis, pairs)  30.8 us
    pallas_call x6, Pallas kernels, call(): pl.pallas_call(kernel, in_specs=[pl.BlockSpec(memory_space=pltpu.SMEM)] +...  15.5 us
  transfers between devices with their start and end apart: 6, of which 2 were waited for; matrix products, arithmetic and copies ran while one was open for 0% of the time, Pallas kernels for 14%

profile of v3, /device:TPU:183, one launch (start us, length us, event | category | flops | bytes accessed | tf_op | source)
XLA Modules:
  0.0 92.2 jit_solution(11664769221650928075)
XLA Ops:
  0.6 0.0 copy-start
  0.6 1.0 %copy-done = bf16[512,512]{1,0:T(8,128)(2,1)S(1)} copy-done((bf16[512,512]{1,0:T(8,128)(2,1)S(1)}, bf16[512,512]{1,0:T(8,128)(2,1)}, u32[]{:S(2)}) %copy-start) | copy-done | bytes 524312
  1.7 0.0 copy-start.2
  1.7 0.7 copy-done.2
  2.4 0.0 copy-start.1
  2.4 0.0 copy-start.4
  2.4 0.1 shard_map.69.own_ref.pair_ref
  2.4 10.8 %collective-permute-start.2 = (bf16[528,512]{1,0:T(8,128)(2,1)S(1)}, bf16[528,512]{1,0:T(8,128)(2,1)S(1)}, u32[]{:S(2)}, u32[]{:S(2)}) collective-permute-start(bf16[528,512]{1,0:T(8,128)(2,1)S(1)} %shard_map.69.own_ref.pair_ref), channel_id=1, source_target_pairs={{0,32},{32,64},{64,96},{96,128},{128,160},{160,192},{192,224},{224... | collective-permute-start | bytes 1622024 | tf_op jit(solution)/shard_map/ppermute | solution.py:18
  13.2 0.0 copy-done.1
  13.2 0.0 copy-done.4
  13.2 0.1 shard_map.68.pair_ref.own_ref
  13.3 0.0 copy-start.3
  13.3 8.2 %collective-permute-start = (bf16[528,512]{1,0:T(8,128)(2,1)S(1)}, bf16[528,512]{1,0:T(8,128)(2,1)S(1)}, u32[]{:S(2)}, u32[]{:S(2)}) collective-permute-start(bf16[528,512]{1,0:T(8,128)(2,1)S(1)} %shard_map.68.pair_ref.own_ref), channel_id=1, source_target_pairs={{0,992},{32,0},{64,32},{96,64},{128,96},{160,128},{192,160},{224,1... | collective-permute-start | bytes 1622024 | tf_op jit(solution)/shard_map/ppermute | solution.py:18
  21.5 3.9 %collective-permute-start.4 = (bf16[528,512]{1,0:T(8,128)(2,1)S(1)}, bf16[528,512]{1,0:T(8,128)(2,1)}, u32[]{:S(2)}, u32[]{:S(2)}) collective-permute-start(bf16[528,512]{1,0:T(8,128)(2,1)S(1)} %shard_map.69.own_ref.pair_ref), channel_id=1, source_target_pairs={{0,1},{1,2},{2,3},{3,4},{4,5},{5,6},{6,7},{7,8},{8,9},{9,10},{10,1... | collective-permute-start | bytes 1622024 | tf_op jit(solution)/shard_map/ppermute | solution.py:18
  25.4 1.9 %collective-permute-start.5 = (bf16[528,512]{1,0:T(8,128)(2,1)S(1)}, bf16[528,512]{1,0:T(8,128)(2,1)S(1)}, u32[]{:S(2)}, u32[]{:S(2)}) collective-permute-start(bf16[528,512]{1,0:T(8,128)(2,1)S(1)} %shard_map.68.pair_ref.own_ref), channel_id=1, source_target_pairs={{0,31},{1,0},{2,1},{3,2},{4,3},{5,4},{6,5},{7,6},{8,7},{9,8},{10,9... | collective-permute-start | bytes 1622024 | tf_op jit(solution)/shard_map/ppermute | solution.py:18
  28.0 0.0 copy-done.3
  28.0 0.1 copy.7.stat_ref
  28.1 0.1 copy.10.stat_ref
  28.3 1.7 %shard_map.71.total_ref = f32[512,512]{1,0:T(8,128)S(1)} custom-call(f32[1,1]{1,0:T(1,128)} %bitcast.6.factor_ref, bf16[528,512]{1,0:T(8,128)(2,1)S(1)} %shard_map.68.pair_ref.own_ref, f32[512,1]{1,0:T(8,128)S(1)} %copy.10.stat_ref, bf16[528,512]{1,0:T(8,128)(2,1)S(1)} %shard_map.69.own_ref.pair_ref), custom_call_target="tpu_custom_call" | custom-call | flops 536870912 | bytes 536870 | tf_op jit(solution)/shard_map/pallas_call | solution.py:100
  30.0 26.3 %collective-permute-done.2.far_ref = bf16[528,512]{1,0:T(8,128)(2,1)S(1)} collective-permute-done((bf16[528,512]{1,0:T(8,128)(2,1)S(1)}, bf16[528,512]{1,0:T(8,128)(2,1)S(1)}, u32[]{:S(2)}, u32[]{:S(2)}) %collective-permute-start.2) | collective-permute-done | bytes 540704 | tf_op jit(solution)/shard_map/ppermute | solution.py:18
  56.2 14.2 %collective-permute-start.3 = (bf16[528,512]{1,0:T(8,128)(2,1)S(1)}, bf16[528,512]{1,0:T(8,128)(2,1)S(1)}, u32[]{:S(2)}, u32[]{:S(2)}) collective-permute-start(bf16[528,512]{1,0:T(8,128)(2,1)S(1)} %collective-permute-done.2.far_ref), channel_id=1, source_target_pairs={{0,1},{1,2},{2,3},{3,4},{4,5},{5,6},{6,7},{7,8},{8,9},{9,10},{10,1... | collective-permute-start | bytes 1622024 | tf_op jit(solution)/shard_map/ppermute | solution.py:18
  70.4 1.7 %shard_map.70.total_ref = f32[512,512]{1,0:T(8,128)S(1)} custom-call(f32[1,1]{1,0:T(1,128)} %bitcast.5.factor_ref, bf16[528,512]{1,0:T(8,128)(2,1)S(1)} %shard_map.69.own_ref.pair_ref, f32[512,1]{1,0:T(8,128)S(1)} %copy.7.stat_ref, bf16[528,512]{1,0:T(8,128)(2,1)S(1)} %shard_map.68.pair_ref.own_ref), custom_call_target="tpu_custom_call" | custom-call | flops 536870912 | bytes 536870 | tf_op jit(solution)/shard_map/pallas_call | solution.py:100
  72.1 4.5 %collective-permute-done.far_ref = bf16[528,512]{1,0:T(8,128)(2,1)S(1)} collective-permute-done((bf16[528,512]{1,0:T(8,128)(2,1)S(1)}, bf16[528,512]{1,0:T(8,128)(2,1)S(1)}, u32[]{:S(2)}, u32[]{:S(2)}) %collective-permute-start) | collective-permute-done | bytes 540704 | tf_op jit(solution)/shard_map/ppermute | solution.py:18
  76.6 3.4 %collective-permute-start.1 = (bf16[528,512]{1,0:T(8,128)(2,1)S(1)}, bf16[528,512]{1,0:T(8,128)(2,1)S(1)}, u32[]{:S(2)}, u32[]{:S(2)}) collective-permute-start(bf16[528,512]{1,0:T(8,128)(2,1)S(1)} %collective-permute-done.far_ref), channel_id=1, source_target_pairs={{0,31},{1,0},{2,1},{3,2},{4,3},{5,4},{6,5},{7,6},{8,7},{9,8},{10,9... | collective-permute-start | bytes 1622024 | tf_op jit(solution)/shard_map/ppermute | solution.py:18
  80.0 0.0 collective-permute-done.4.near_ref
  80.0 4.2 %shard_map.72.total_ref = f32[512,512]{1,0:T(8,128)S(1)} custom-call(f32[1,1]{1,0:T(1,128)} %bitcast.7.factor_ref, bf16[528,512]{1,0:T(8,128)(2,1)S(1)} %shard_map.68.pair_ref.own_ref, f32[512,1]{1,0:T(8,128)S(1)} %copy.10.stat_ref, bf16[528,512]{1,0:T(8,128)(2,1)} %collective-permute-done.4.near_ref, bf16[528,512]{1,0:T(8,128)(2,1)S(1)} %collective-permute-done.2.far_ref, ...), custom_call_target="tpu_custom_call" | custom-call | flops 1073741824 | bytes 1073741 | tf_op jit(solution)/shard_map/pallas_call | solution.py:100
  84.2 0.0 collective-permute-done.5.near_ref
  84.2 3.1 %shard_map.74.total_ref = f32[512,512]{1,0:T(8,128)S(1)} custom-call(f32[1,1]{1,0:T(1,128)} %bitcast.9.factor_ref, bf16[528,512]{1,0:T(8,128)(2,1)S(1)} %shard_map.69.own_ref.pair_ref, f32[512,1]{1,0:T(8,128)S(1)} %copy.7.stat_ref, bf16[528,512]{1,0:T(8,128)(2,1)S(1)} %collective-permute-done.5.near_ref, bf16[528,512]{1,0:T(8,128)(2,1)S(1)} %collective-permute-done.far_ref, ...), custom_call_target="tpu_custom_call" | custom-call | flops 1073741824 | bytes 1073741 | tf_op jit(solution)/shard_map/pallas_call | solution.py:100
  87.3 0.0 collective-permute-done.3.both_ref
  87.4 2.4 %shard_map.73 = f32[512,512]{1,0:T(8,128)} custom-call(f32[1,1]{1,0:T(1,128)} %bitcast.8.factor_ref, bf16[528,512]{1,0:T(8,128)(2,1)S(1)} %shard_map.68.pair_ref.own_ref, f32[512,1]{1,0:T(8,128)S(1)} %copy.10.stat_ref, bf16[528,512]{1,0:T(8,128)(2,1)S(1)} %collective-permute-done.3.both_ref, f32[512,512]{1,0:T(8,128)S(1)} %shard_map.72.total_ref), custom_call_target="tpu_custom_call" | custom-call | flops 536870912 | bytes 536870 | tf_op jit(solution)/shard_map/pallas_call | solution.py:100
  89.8 0.0 collective-permute-done.1.both_ref
  89.8 2.4 %shard_map.75 = f32[512,512]{1,0:T(8,128)} custom-call(f32[1,1]{1,0:T(1,128)} %bitcast.10.factor_ref, bf16[528,512]{1,0:T(8,128)(2,1)S(1)} %shard_map.69.own_ref.pair_ref, f32[512,1]{1,0:T(8,128)S(1)} %copy.7.stat_ref, bf16[528,512]{1,0:T(8,128)(2,1)S(1)} %collective-permute-done.1.both_ref, f32[512,512]{1,0:T(8,128)S(1)} %shard_map.74.total_ref), custom_call_target="tpu_custom_call" | custom-call | flops 536870912 | bytes 536870 | tf_op jit(solution)/shard_map/pallas_call | solution.py:100
Async XLA Ops:
  0.6 1.0 %copy-start = (bf16[512,512]{1,0:T(8,128)(2,1)S(1)}, bf16[512,512]{1,0:T(8,128)(2,1)}, u32[]{:S(2)}) copy-start(bf16[512,512]{1,0:T(8,128)(2,1)} %rows_ref.3) | copy-start | bytes 1572868
  1.7 0.7 copy-start.2
  2.4 10.9 %copy-start.1 = (bf16[512,512]{1,0:T(8,128)(2,1)S(1)}, bf16[512,512]{1,0:T(8,128)(2,1)}, u32[]{:S(2)}) copy-start(bf16[512,512]{1,0:T(8,128)(2,1)} %rows_ref.2) | copy-start | bytes 1572868
  2.4 10.9 %copy-start.4 = (f32[512]{0:T(512)S(1)}, f32[512]{0:T(512)}, u32[]{:S(2)}) copy-start(f32[512]{0:T(512)} %param.7) | copy-start | bytes 6148
  2.4 53.8 %collective-permute-start.2 = (bf16[528,512]{1,0:T(8,128)(2,1)S(1)}, bf16[528,512]{1,0:T(8,128)(2,1)S(1)}, u32[]{:S(2)}, u32[]{:S(2)}) collective-permute-start(bf16[528,512]{1,0:T(8,128)(2,1)S(1)} %shard_map.69.own_ref.pair_ref), channel_id=1, source_target_pairs={{0,32},{32,64},{64,96},{96,128},{128,160},{160,192},{192,224},{224... | collective-permute-start | bytes 1622024 | tf_op jit(solution)/shard_map/ppermute | solution.py:18
  13.3 14.6 %copy-start.3 = (f32[512]{0:T(512)S(1)}, f32[512]{0:T(512)}, u32[]{:S(2)}) copy-start(f32[512]{0:T(512)} %param.8) | copy-start | bytes 6148
  13.3 63.2 %collective-permute-start = (bf16[528,512]{1,0:T(8,128)(2,1)S(1)}, bf16[528,512]{1,0:T(8,128)(2,1)S(1)}, u32[]{:S(2)}, u32[]{:S(2)}) collective-permute-start(bf16[528,512]{1,0:T(8,128)(2,1)S(1)} %shard_map.68.pair_ref.own_ref), channel_id=1, source_target_pairs={{0,992},{32,0},{64,32},{96,64},{128,96},{160,128},{192,160},{224,1... | collective-permute-start | bytes 1622024 | tf_op jit(solution)/shard_map/ppermute | solution.py:18
  21.5 58.5 %collective-permute-start.4 = (bf16[528,512]{1,0:T(8,128)(2,1)S(1)}, bf16[528,512]{1,0:T(8,128)(2,1)}, u32[]{:S(2)}, u32[]{:S(2)}) collective-permute-start(bf16[528,512]{1,0:T(8,128)(2,1)S(1)} %shard_map.69.own_ref.pair_ref), channel_id=1, source_target_pairs={{0,1},{1,2},{2,3},{3,4},{4,5},{5,6},{6,7},{7,8},{8,9},{9,10},{10,1... | collective-permute-start | bytes 1622024 | tf_op jit(solution)/shard_map/ppermute | solution.py:18
  25.4 58.8 %collective-permute-start.5 = (bf16[528,512]{1,0:T(8,128)(2,1)S(1)}, bf16[528,512]{1,0:T(8,128)(2,1)S(1)}, u32[]{:S(2)}, u32[]{:S(2)}) collective-permute-start(bf16[528,512]{1,0:T(8,128)(2,1)S(1)} %shard_map.68.pair_ref.own_ref), channel_id=1, source_target_pairs={{0,31},{1,0},{2,1},{3,2},{4,3},{5,4},{6,5},{7,6},{8,7},{9,8},{10,9... | collective-permute-start | bytes 1622024 | tf_op jit(solution)/shard_map/ppermute | solution.py:18
  56.2 31.1 %collective-permute-start.3 = (bf16[528,512]{1,0:T(8,128)(2,1)S(1)}, bf16[528,512]{1,0:T(8,128)(2,1)S(1)}, u32[]{:S(2)}, u32[]{:S(2)}) collective-permute-start(bf16[528,512]{1,0:T(8,128)(2,1)S(1)} %collective-permute-done.2.far_ref), channel_id=1, source_target_pairs={{0,1},{1,2},{2,3},{3,4},{4,5},{5,6},{6,7},{7,8},{8,9},{9,10},{10,1... | collective-permute-start | bytes 1622024 | tf_op jit(solution)/shard_map/ppermute | solution.py:18
  76.6 13.2 %collective-permute-start.1 = (bf16[528,512]{1,0:T(8,128)(2,1)S(1)}, bf16[528,512]{1,0:T(8,128)(2,1)S(1)}, u32[]{:S(2)}, u32[]{:S(2)}) collective-permute-start(bf16[528,512]{1,0:T(8,128)(2,1)S(1)} %collective-permute-done.far_ref), channel_id=1, source_target_pairs={{0,31},{1,0},{2,1},{3,2},{4,3},{5,4},{6,5},{7,6},{8,7},{9,8},{10,9... | collective-permute-start | bytes 1622024 | tf_op jit(solution)/shard_map/ppermute | solution.py:18

commit v4 on v3

--- a/solution.py
+++ b/solution.py
@@ -6,10 +6,10 @@
 from jax.sharding import PartitionSpec as P
 
 STAT_ROWS = 16
-BLOCKS = 4
+BLOCKS = 2
 VMEM_BYTES = 16 * 1024 * 1024
 PACK_VMEM_BYTES = 8 * 1024 * 1024
-COSTS = (2**29, 2**30, 2**29)
+COSTS = (2**29, 2**29, 2**29, 2**29)
 
 
 def shifted(value, axis, steps):
@@ -53,16 +53,23 @@
     return [pl.ds(k * size, size) for k in range(BLOCKS)]
 
 
-def tile_term(factor, own, own_stat, packed_ref):
+def tile_weights(factor, own, own_stat, packed_ref):
     rows = packed_ref.shape[0] - STAT_ROWS
-    other = packed_ref[pl.ds(0, rows), :]
     pieces = packed_ref[pl.ds(rows, STAT_ROWS), :].astype(jnp.float32)
     other_stat = pieces[0:1, :] + (pieces[1:2, :] + pieces[2:3, :])
     scores = factor * lax.dot_general(
-        own, other, (((1,), (1,)), ((), ())), preferred_element_type=jnp.float32
+        own,
+        packed_ref[pl.ds(0, rows), :],
+        (((1,), (1,)), ((), ())),
+        preferred_element_type=jnp.float32,
     )
-    weights = (jnp.exp(scores - own_stat) + jnp.exp(scores - other_stat)).astype(jnp.bfloat16)
-    return jnp.dot(weights, other, preferred_element_type=jnp.float32)
+    return (jnp.exp(scores - own_stat) + jnp.exp(scores - other_stat)).astype(jnp.bfloat16)
+
+
+def tile_term(factor, own, own_stat, packed_ref):
+    rows = packed_ref.shape[0] - STAT_ROWS
+    weights = tile_weights(factor, own, own_stat, packed_ref)
+    return jnp.dot(weights, packed_ref[pl.ds(0, rows), :], preferred_element_type=jnp.float32)
 
 
 def first_kernel(factor_ref, own_ref, stat_ref, pair_ref, out_ref):
@@ -72,22 +79,30 @@
         out_ref[cut, :] = term - 2.0 * pair_ref[cut, :].astype(jnp.float32)
 
 
-def middle_kernel(factor_ref, own_ref, stat_ref, near_ref, far_ref, total_ref, out_ref):
+def middle_kernel(factor_ref, own_ref, stat_ref, other_ref, total_ref, out_ref):
     factor = factor_ref[0, 0]
     for cut in blocks(own_ref):
-        own, stat = own_ref[cut, :], stat_ref[cut, :]
-        total = total_ref[cut, :] + tile_term(factor, own, stat, near_ref)
-        out_ref[cut, :] = total + tile_term(factor, own, stat, far_ref)
+        term = tile_term(factor, own_ref[cut, :], stat_ref[cut, :], other_ref)
+        out_ref[cut, :] = total_ref[cut, :] + term
 
 
 def last_kernel(factor_ref, own_ref, stat_ref, both_ref, total_ref, out_ref, done, sems):
     factor = factor_ref[0, 0]
+    rows, width = done.shape
     copies = []
     for k, cut in enumerate(blocks(own_ref)):
-        term = tile_term(factor, own_ref[cut, :], stat_ref[cut, :], both_ref)
-        done[cut, :] = factor * (total_ref[cut, :] + term)
-        copies.append(pltpu.make_async_copy(done.at[cut, :], out_ref.at[cut, :], sems.at[k]))
-        copies[k].start()
+        weights = tile_weights(factor, own_ref[cut, :], stat_ref[cut, :], both_ref)
+        for half in range(2):
+            part = pl.ds(half * (width // 2), width // 2)
+            term = jnp.dot(
+                weights, both_ref[pl.ds(0, rows), part], preferred_element_type=jnp.float32
+            )
+            done[cut, part] = factor * (total_ref[cut, part] + term)
+            copy = pltpu.make_async_copy(
+                done.at[cut, part], out_ref.at[cut, part], sems.at[2 * k + half]
+            )
+            copy.start()
+            copies.append(copy)
     for copy in copies:
         copy.wait()
 
@@ -96,7 +111,7 @@
     rows, width = stat.shape[0], own.shape[1]
     vmem = pl.BlockSpec(memory_space=pltpu.VMEM)
     last = kernel is last_kernel
-    scratch = [pltpu.VMEM((rows, width), jnp.float32), pltpu.SemaphoreType.DMA((BLOCKS,))]
+    scratch = [pltpu.VMEM((rows, width), jnp.float32), pltpu.SemaphoreType.DMA((2 * BLOCKS,))]
     return pl.pallas_call(
         kernel,
         in_specs=[pl.BlockSpec(memory_space=pltpu.SMEM)] + [vmem] * (2 + len(arrays)),
@@ -125,14 +140,18 @@
     image_total = call(first_kernel, COSTS[0], *on_images, text)
     text_total = call(first_kernel, COSTS[0], *on_texts, image)
     far_text, image_total = lax.optimization_barrier((far_text, image_total))
-    far_image, text_total = lax.optimization_barrier((far_image, text_total))
     both_text = shifted(far_text, "inner", 1)
+    image_total = call(middle_kernel, COSTS[1], *on_images, far_text, image_total)
+    far_image, image_total, text_total = lax.optimization_barrier(
+        (far_image, image_total, text_total)
+    )
     both_image = shifted(far_image, "inner", -1)
-    image_total = call(middle_kernel, COSTS[1], *on_images, near_text, far_text, image_total)
-    text_total = call(middle_kernel, COSTS[1], *on_texts, near_image, far_image, text_total)
-    image_grad = call(last_kernel, COSTS[2], *on_images, both_text, image_total)
+    image_total = call(middle_kernel, COSTS[1], *on_images, near_text, image_total)
+    text_total = call(middle_kernel, COSTS[1], *on_texts, near_image, text_total)
+    text_total = call(middle_kernel, COSTS[2], *on_texts, far_image, text_total)
+    image_grad = call(last_kernel, COSTS[3], *on_images, both_text, image_total)
     both_image, image_grad = lax.optimization_barrier((both_image, image_grad))
-    text_grad = call(last_kernel, COSTS[2], *on_texts, both_image, text_total)
+    text_grad = call(last_kernel, COSTS[3], *on_texts, both_image, text_total)
     return (image_grad, text_grad)
 
 

time: 92.6 us -> 91.6 us (0.989)
  Pallas kernels: 15.6 us -> 11.1 us
  starting transfers between devices: 42.3 us -> 44.2 us
  waiting for transfers between devices: 30.8 us -> 31.8 us
    pallas_call x6 -> x8, Pallas kernels: 15.5 us -> 11 us  [call(): pl.pallas_call(kernel, in_specs=[pl.BlockSpec(memory_space=pltpu.SMEM)] +...]
    ppermute x6, starting transfers between devices: 42.3 us -> 44.2 us  [shifted(): return lax.ppermute(value, axis, pairs)]
    ppermute x6, waiting for transfers between devices: 30.8 us -> 31.8 us  [shifted(): return lax.ppermute(value, axis, pairs)]
  transfers between devices with their start and end apart: 6 -> 6, of which waited for: 2 -> 3; matrix products, arithmetic and copies ran while one was open for 0% -> 0% of each run, Pallas kernels for 14% -> 10%
where the time goes in v4:
time: 91.6 us; the launch traced here: 91.2 us
  starting transfers between devices  44.2 us (48%)
  waiting for transfers between devices  31.8 us (35%)
  Pallas kernels  11.1 us (12%)
  local copies, waits for them, and re-layouts  2.54 us (3%)
  between operations  1.47 us (2%)
    ppermute x6, starting transfers between devices, shifted(): return lax.ppermute(value, axis, pairs)  44.2 us
    ppermute x6, waiting for transfers between devices, shifted(): return lax.ppermute(value, axis, pairs)  31.8 us
    pallas_call x8, Pallas kernels, call(): pl.pallas_call(kernel, in_specs=[pl.BlockSpec(memory_space=pltpu.SMEM)] +...  11 us
    unnamed x10, local copies, waits for them, and re-layouts  2.25 us
  transfers between devices with their start and end apart: 6, of which 3 were waited for; matrix products, arithmetic and copies ran while one was open for 0% of the time, Pallas kernels for 10%

profile of v4, /device:TPU:183, one launch (start us, length us, event | category | flops | bytes accessed | tf_op | source)
XLA Modules:
  0.0 91.2 jit_solution(12963017175841569185)
XLA Ops:
  0.6 0.0 copy-start
  0.6 1.0 %copy-done = bf16[512,512]{1,0:T(8,128)(2,1)S(1)} copy-done((bf16[512,512]{1,0:T(8,128)(2,1)S(1)}, bf16[512,512]{1,0:T(8,128)(2,1)}, u32[]{:S(2)}) %copy-start) | copy-done | bytes 524312
  1.7 0.0 copy-start.3
  1.7 0.7 copy-done.3
  2.4 0.0 copy-start.1
  2.4 0.0 copy-start.2
  2.4 0.1 shard_map.69.pair_ref.own_ref
  2.4 10.8 %collective-permute-start.1 = (bf16[528,512]{1,0:T(8,128)(2,1)S(1)}, bf16[528,512]{1,0:T(8,128)(2,1)S(1)}, u32[]{:S(2)}, u32[]{:S(2)}) collective-permute-start(bf16[528,512]{1,0:T(8,128)(2,1)S(1)} %shard_map.69.pair_ref.own_ref), channel_id=1, source_target_pairs={{0,32},{32,64},{64,96},{96,128},{128,160},{160,192},{192,224},{224... | collective-permute-start | bytes 1622024 | tf_op jit(solution)/shard_map/ppermute | solution.py:18
  13.2 0.0 copy-done.1
  13.2 0.0 copy-done.2
  13.2 0.1 shard_map.68.own_ref.pair_ref
  13.3 8.2 %collective-permute-start = (bf16[528,512]{1,0:T(8,128)(2,1)S(1)}, bf16[528,512]{1,0:T(8,128)(2,1)S(1)}, u32[]{:S(2)}, u32[]{:S(2)}) collective-permute-start(bf16[528,512]{1,0:T(8,128)(2,1)S(1)} %shard_map.68.own_ref.pair_ref), channel_id=1, source_target_pairs={{0,992},{32,0},{64,32},{96,64},{128,96},{160,128},{192,160},{224,1... | collective-permute-start | bytes 1622024 | tf_op jit(solution)/shard_map/ppermute | solution.py:18
  21.5 2.9 %collective-permute-start.5 = (bf16[528,512]{1,0:T(8,128)(2,1)S(1)}, bf16[528,512]{1,0:T(8,128)(2,1)}, u32[]{:S(2)}, u32[]{:S(2)}) collective-permute-start(bf16[528,512]{1,0:T(8,128)(2,1)S(1)} %shard_map.68.own_ref.pair_ref), channel_id=1, source_target_pairs={{0,31},{1,0},{2,1},{3,2},{4,3},{5,4},{6,5},{7,6},{8,7},{9,8},{10,9... | collective-permute-start | bytes 1622024 | tf_op jit(solution)/shard_map/ppermute | solution.py:18
  24.4 4.8 %collective-permute-start.4 = (bf16[528,512]{1,0:T(8,128)(2,1)S(1)}, bf16[528,512]{1,0:T(8,128)(2,1)S(1)}, u32[]{:S(2)}, u32[]{:S(2)}) collective-permute-start(bf16[528,512]{1,0:T(8,128)(2,1)S(1)} %shard_map.69.pair_ref.own_ref), channel_id=1, source_target_pairs={{0,1},{1,2},{2,3},{3,4},{4,5},{5,6},{6,7},{7,8},{8,9},{9,10},{10,1... | collective-permute-start | bytes 1622024 | tf_op jit(solution)/shard_map/ppermute | solution.py:18
  29.8 0.0 copy-start.4
  29.8 0.1 copy.8.stat_ref
  30.0 0.5 copy-done.4
  30.5 0.1 copy.9.stat_ref
  30.7 1.0 %shard_map.70.total_ref = f32[512,512]{1,0:T(8,128)S(1)} custom-call(f32[1,1]{1,0:T(1,128)} %bitcast.5.factor_ref, bf16[528,512]{1,0:T(8,128)(2,1)S(1)} %shard_map.68.own_ref.pair_ref, f32[512,1]{1,0:T(8,128)S(1)} %copy.8.stat_ref, bf16[528,512]{1,0:T(8,128)(2,1)S(1)} %shard_map.69.pair_ref.own_ref), custom_call_target="tpu_custom_call" | custom-call | flops 536870912 | bytes 536870 | tf_op jit(solution)/shard_map/pallas_call | solution.py:115
  31.7 1.0 %shard_map.72.total_ref = f32[512,512]{1,0:T(8,128)S(1)} custom-call(f32[1,1]{1,0:T(1,128)} %bitcast.7.factor_ref, bf16[528,512]{1,0:T(8,128)(2,1)S(1)} %shard_map.69.pair_ref.own_ref, f32[512,1]{1,0:T(8,128)S(1)} %copy.9.stat_ref, bf16[528,512]{1,0:T(8,128)(2,1)S(1)} %shard_map.68.own_ref.pair_ref), custom_call_target="tpu_custom_call" | custom-call | flops 536870912 | bytes 536870 | tf_op jit(solution)/shard_map/pallas_call | solution.py:115
  32.7 23.5 %collective-permute-done.1.other_ref = bf16[528,512]{1,0:T(8,128)(2,1)S(1)} collective-permute-done((bf16[528,512]{1,0:T(8,128)(2,1)S(1)}, bf16[528,512]{1,0:T(8,128)(2,1)S(1)}, u32[]{:S(2)}, u32[]{:S(2)}) %collective-permute-start.1) | collective-permute-done | bytes 540704 | tf_op jit(solution)/shard_map/ppermute | solution.py:18
  56.2 14.2 %collective-permute-start.3 = (bf16[528,512]{1,0:T(8,128)(2,1)S(1)}, bf16[528,512]{1,0:T(8,128)(2,1)S(1)}, u32[]{:S(2)}, u32[]{:S(2)}) collective-permute-start(bf16[528,512]{1,0:T(8,128)(2,1)S(1)} %collective-permute-done.1.other_ref), channel_id=1, source_target_pairs={{0,1},{1,2},{2,3},{3,4},{4,5},{5,6},{6,7},{7,8},{8,9},{9,10},{10,1... | collective-permute-start | bytes 1622024 | tf_op jit(solution)/shard_map/ppermute | solution.py:18
  70.4 1.0 %shard_map.71.total_ref = f32[512,512]{1,0:T(8,128)S(1)} custom-call(f32[1,1]{1,0:T(1,128)} %bitcast.6.factor_ref, bf16[528,512]{1,0:T(8,128)(2,1)S(1)} %shard_map.68.own_ref.pair_ref, f32[512,1]{1,0:T(8,128)S(1)} %copy.8.stat_ref, bf16[528,512]{1,0:T(8,128)(2,1)S(1)} %collective-permute-done.1.other_ref, f32[512,512]{1,0:T(8,128)S(1)} %shard_map.70.total_ref), custom_call_target="tpu_custom_call" | custom-call | flops 536870912 | bytes 536870 | tf_op jit(solution)/shard_map/pallas_call | solution.py:115
  71.5 5.1 %collective-permute-done.other_ref = bf16[528,512]{1,0:T(8,128)(2,1)S(1)} collective-permute-done((bf16[528,512]{1,0:T(8,128)(2,1)S(1)}, bf16[528,512]{1,0:T(8,128)(2,1)S(1)}, u32[]{:S(2)}, u32[]{:S(2)}) %collective-permute-start) | collective-permute-done | bytes 540704 | tf_op jit(solution)/shard_map/ppermute | solution.py:18
  76.5 3.4 %collective-permute-start.2 = (bf16[528,512]{1,0:T(8,128)(2,1)S(1)}, bf16[528,512]{1,0:T(8,128)(2,1)S(1)}, u32[]{:S(2)}, u32[]{:S(2)}) collective-permute-start(bf16[528,512]{1,0:T(8,128)(2,1)S(1)} %collective-permute-done.other_ref), channel_id=1, source_target_pairs={{0,31},{1,0},{2,1},{3,2},{4,3},{5,4},{6,5},{7,6},{8,7},{9,8},{10,9... | collective-permute-start | bytes 1622024 | tf_op jit(solution)/shard_map/ppermute | solution.py:18
  80.0 0.0 collective-permute-done.5.other_ref
  80.0 2.1 %shard_map.75.total_ref = f32[512,512]{1,0:T(8,128)S(1)} custom-call(f32[1,1]{1,0:T(1,128)} %bitcast.10.factor_ref, bf16[528,512]{1,0:T(8,128)(2,1)S(1)} %shard_map.69.pair_ref.own_ref, f32[512,1]{1,0:T(8,128)S(1)} %copy.9.stat_ref, bf16[528,512]{1,0:T(8,128)(2,1)} %collective-permute-done.5.other_ref, f32[512,512]{1,0:T(8,128)S(1)} %shard_map.72.total_ref), custom_call_target="tpu_custom_call" | custom-call | flops 536870912 | bytes 536870 | tf_op jit(solution)/shard_map/pallas_call | solution.py:115
  82.1 1.0 %shard_map.76.total_ref = f32[512,512]{1,0:T(8,128)S(1)} custom-call(f32[1,1]{1,0:T(1,128)} %bitcast.11.factor_ref, bf16[528,512]{1,0:T(8,128)(2,1)S(1)} %shard_map.69.pair_ref.own_ref, f32[512,1]{1,0:T(8,128)S(1)} %copy.9.stat_ref, bf16[528,512]{1,0:T(8,128)(2,1)S(1)} %collective-permute-done.other_ref, f32[512,512]{1,0:T(8,128)S(1)} %shard_map.75.total_ref), custom_call_target="tpu_custom_call" | custom-call | flops 536870912 | bytes 536870 | tf_op jit(solution)/shard_map/pallas_call | solution.py:115
  83.1 0.0 collective-permute-done.4.other_ref
  83.1 1.0 %shard_map.73.total_ref = f32[512,512]{1,0:T(8,128)S(1)} custom-call(f32[1,1]{1,0:T(1,128)} %bitcast.8.factor_ref, bf16[528,512]{1,0:T(8,128)(2,1)S(1)} %shard_map.68.own_ref.pair_ref, f32[512,1]{1,0:T(8,128)S(1)} %copy.8.stat_ref, bf16[528,512]{1,0:T(8,128)(2,1)S(1)} %collective-permute-done.4.other_ref, f32[512,512]{1,0:T(8,128)S(1)} %shard_map.71.total_ref), custom_call_target="tpu_custom_call" | custom-call | flops 536870912 | bytes 536870 | tf_op jit(solution)/shard_map/pallas_call | solution.py:115
  84.2 0.0 collective-permute-done.3.both_ref
  84.2 1.9 %shard_map.74 = f32[512,512]{1,0:T(8,128)} custom-call(f32[1,1]{1,0:T(1,128)} %bitcast.9.factor_ref, bf16[528,512]{1,0:T(8,128)(2,1)S(1)} %shard_map.68.own_ref.pair_ref, f32[512,1]{1,0:T(8,128)S(1)} %copy.8.stat_ref, bf16[528,512]{1,0:T(8,128)(2,1)S(1)} %collective-permute-done.3.both_ref, f32[512,512]{1,0:T(8,128)S(1)} %shard_map.73.total_ref), custom_call_target="tpu_custom_call" | custom-call | flops 536870912 | bytes 536870 | tf_op jit(solution)/shard_map/pallas_call | solution.py:115
  86.1 3.3 %collective-permute-done.2.both_ref = bf16[528,512]{1,0:T(8,128)(2,1)S(1)} collective-permute-done((bf16[528,512]{1,0:T(8,128)(2,1)S(1)}, bf16[528,512]{1,0:T(8,128)(2,1)S(1)}, u32[]{:S(2)}, u32[]{:S(2)}) %collective-permute-start.2) | collective-permute-done | bytes 540704 | tf_op jit(solution)/shard_map/ppermute | solution.py:18
  89.3 1.9 %shard_map.77 = f32[512,512]{1,0:T(8,128)} custom-call(f32[1,1]{1,0:T(1,128)} %bitcast.12.factor_ref, bf16[528,512]{1,0:T(8,128)(2,1)S(1)} %shard_map.69.pair_ref.own_ref, f32[512,1]{1,0:T(8,128)S(1)} %copy.9.stat_ref, bf16[528,512]{1,0:T(8,128)(2,1)S(1)} %collective-permute-done.2.both_ref, f32[512,512]{1,0:T(8,128)S(1)} %shard_map.76.total_ref), custom_call_target="tpu_custom_call" | custom-call | flops 536870912 | bytes 536870 | tf_op jit(solution)/shard_map/pallas_call | solution.py:115
Async XLA Ops:
  0.6 1.0 %copy-start = (bf16[512,512]{1,0:T(8,128)(2,1)S(1)}, bf16[512,512]{1,0:T(8,128)(2,1)}, u32[]{:S(2)}) copy-start(bf16[512,512]{1,0:T(8,128)(2,1)} %rows_ref.3) | copy-start | bytes 1572868
  1.7 0.7 copy-start.3
  2.4 10.9 %copy-start.1 = (bf16[512,512]{1,0:T(8,128)(2,1)S(1)}, bf16[512,512]{1,0:T(8,128)(2,1)}, u32[]{:S(2)}) copy-start(bf16[512,512]{1,0:T(8,128)(2,1)} %rows_ref.2) | copy-start | bytes 1572868
  2.4 10.9 %copy-start.2 = (f32[512]{0:T(512)S(1)}, f32[512]{0:T(512)}, u32[]{:S(2)}) copy-start(f32[512]{0:T(512)} %param.7) | copy-start | bytes 6148
  2.4 53.8 %collective-permute-start.1 = (bf16[528,512]{1,0:T(8,128)(2,1)S(1)}, bf16[528,512]{1,0:T(8,128)(2,1)S(1)}, u32[]{:S(2)}, u32[]{:S(2)}) collective-permute-start(bf16[528,512]{1,0:T(8,128)(2,1)S(1)} %shard_map.69.pair_ref.own_ref), channel_id=1, source_target_pairs={{0,32},{32,64},{64,96},{96,128},{128,160},{160,192},{192,224},{224... | collective-permute-start | bytes 1622024 | tf_op jit(solution)/shard_map/ppermute | solution.py:18
  13.3 63.2 %collective-permute-start = (bf16[528,512]{1,0:T(8,128)(2,1)S(1)}, bf16[528,512]{1,0:T(8,128)(2,1)S(1)}, u32[]{:S(2)}, u32[]{:S(2)}) collective-permute-start(bf16[528,512]{1,0:T(8,128)(2,1)S(1)} %shard_map.68.own_ref.pair_ref), channel_id=1, source_target_pairs={{0,992},{32,0},{64,32},{96,64},{128,96},{160,128},{192,160},{224,1... | collective-permute-start | bytes 1622024 | tf_op jit(solution)/shard_map/ppermute | solution.py:18
  21.5 58.5 %collective-permute-start.5 = (bf16[528,512]{1,0:T(8,128)(2,1)S(1)}, bf16[528,512]{1,0:T(8,128)(2,1)}, u32[]{:S(2)}, u32[]{:S(2)}) collective-permute-start(bf16[528,512]{1,0:T(8,128)(2,1)S(1)} %shard_map.68.own_ref.pair_ref), channel_id=1, source_target_pairs={{0,31},{1,0},{2,1},{3,2},{4,3},{5,4},{6,5},{7,6},{8,7},{9,8},{10,9... | collective-permute-start | bytes 1622024 | tf_op jit(solution)/shard_map/ppermute | solution.py:18
  24.4 58.7 %collective-permute-start.4 = (bf16[528,512]{1,0:T(8,128)(2,1)S(1)}, bf16[528,512]{1,0:T(8,128)(2,1)S(1)}, u32[]{:S(2)}, u32[]{:S(2)}) collective-permute-start(bf16[528,512]{1,0:T(8,128)(2,1)S(1)} %shard_map.69.pair_ref.own_ref), channel_id=1, source_target_pairs={{0,1},{1,2},{2,3},{3,4},{4,5},{5,6},{6,7},{7,8},{8,9},{9,10},{10,1... | collective-permute-start | bytes 1622024 | tf_op jit(solution)/shard_map/ppermute | solution.py:18
  29.8 0.7 copy-start.4
  56.2 28.0 %collective-permute-start.3 = (bf16[528,512]{1,0:T(8,128)(2,1)S(1)}, bf16[528,512]{1,0:T(8,128)(2,1)S(1)}, u32[]{:S(2)}, u32[]{:S(2)}) collective-permute-start(bf16[528,512]{1,0:T(8,128)(2,1)S(1)} %collective-permute-done.1.other_ref), channel_id=1, source_target_pairs={{0,1},{1,2},{2,3},{3,4},{4,5},{5,6},{6,7},{7,8},{8,9},{9,10},{10,1... | collective-permute-start | bytes 1622024 | tf_op jit(solution)/shard_map/ppermute | solution.py:18
  76.5 12.8 %collective-permute-start.2 = (bf16[528,512]{1,0:T(8,128)(2,1)S(1)}, bf16[528,512]{1,0:T(8,128)(2,1)S(1)}, u32[]{:S(2)}, u32[]{:S(2)}) collective-permute-start(bf16[528,512]{1,0:T(8,128)(2,1)S(1)} %collective-permute-done.other_ref), channel_id=1, source_target_pairs={{0,31},{1,0},{2,1},{3,2},{4,3},{5,4},{6,5},{7,6},{8,7},{9,8},{10,9... | collective-permute-start | bytes 1622024 | tf_op jit(solution)/shard_map/ppermute | solution.py:18

commit v5 on v4

--- a/solution.py
+++ b/solution.py
@@ -139,16 +139,15 @@
     on_texts = (factor, text, text_lse.reshape(rows, 1))
     image_total = call(first_kernel, COSTS[0], *on_images, text)
     text_total = call(first_kernel, COSTS[0], *on_texts, image)
-    far_text, image_total = lax.optimization_barrier((far_text, image_total))
+    far_text, image_total, text_total = lax.optimization_barrier(
+        (far_text, image_total, text_total)
+    )
     both_text = shifted(far_text, "inner", 1)
-    image_total = call(middle_kernel, COSTS[1], *on_images, far_text, image_total)
-    far_image, image_total, text_total = lax.optimization_barrier(
-        (far_image, image_total, text_total)
-    )
     both_image = shifted(far_image, "inner", -1)
     image_total = call(middle_kernel, COSTS[1], *on_images, near_text, image_total)
     text_total = call(middle_kernel, COSTS[1], *on_texts, near_image, text_total)
-    text_total = call(middle_kernel, COSTS[2], *on_texts, far_image, text_total)
+    image_total = call(middle_kernel, COSTS[1], *on_images, far_text, image_total)
+    text_total = call(middle_kernel, COSTS[1], *on_texts, far_image, text_total)
     image_grad = call(last_kernel, COSTS[3], *on_images, both_text, image_total)
     both_image, image_grad = lax.optimization_barrier((both_image, image_grad))
     text_grad = call(last_kernel, COSTS[3], *on_texts, both_image, text_total)

time: 91.6 us -> 91.6 us (level)
  starting transfers between devices: 44.2 us -> 42.3 us
  waiting for transfers between devices: 31.8 us -> 33.7 us
    ppermute x6, waiting for transfers between devices: 31.8 us -> 33.7 us  [shifted(): return lax.ppermute(value, axis, pairs)]
    ppermute x6, starting transfers between devices: 44.2 us -> 42.3 us  [shifted(): return lax.ppermute(value, axis, pairs)]
where the time goes in v5:
time: 91.6 us; the launch traced here: 91.2 us
  starting transfers between devices  42.3 us (46%)
  waiting for transfers between devices  33.7 us (37%)
  Pallas kernels  11.1 us (12%)
  local copies, waits for them, and re-layouts  2.54 us (3%)
  between operations  1.47 us (2%)
    ppermute x6, starting transfers between devices, shifted(): return lax.ppermute(value, axis, pairs)  42.3 us
    ppermute x6, waiting for transfers between devices, shifted(): return lax.ppermute(value, axis, pairs)  33.7 us
    pallas_call x8, Pallas kernels, call(): pl.pallas_call(kernel, in_specs=[pl.BlockSpec(memory_space=pltpu.SMEM)] +...  11 us
    unnamed x10, local copies, waits for them, and re-layouts  2.25 us
  transfers between devices with their start and end apart: 6, of which 3 were waited for; matrix products, arithmetic and copies ran while one was open for 0% of the time, Pallas kernels for 10%

profile of v5, /device:TPU:183, one launch (start us, length us, event | category | flops | bytes accessed | tf_op | source)
XLA Modules:
  0.0 91.2 jit_solution(11910036166334569181)
XLA Ops:
  0.6 0.0 copy-start
  0.6 1.0 %copy-done = bf16[512,512]{1,0:T(8,128)(2,1)S(1)} copy-done((bf16[512,512]{1,0:T(8,128)(2,1)S(1)}, bf16[512,512]{1,0:T(8,128)(2,1)}, u32[]{:S(2)}) %copy-start) | copy-done | bytes 524312
  1.7 0.0 copy-start.3
  1.7 0.7 copy-done.3
  2.4 0.0 copy-start.1
  2.4 0.0 copy-start.2
  2.4 0.1 shard_map.69.pair_ref.own_ref
  2.4 10.8 %collective-permute-start.2 = (bf16[528,512]{1,0:T(8,128)(2,1)S(1)}, bf16[528,512]{1,0:T(8,128)(2,1)S(1)}, u32[]{:S(2)}, u32[]{:S(2)}) collective-permute-start(bf16[528,512]{1,0:T(8,128)(2,1)S(1)} %shard_map.69.pair_ref.own_ref), channel_id=1, source_target_pairs={{0,32},{32,64},{64,96},{96,128},{128,160},{160,192},{192,224},{224... | collective-permute-start | bytes 1622024 | tf_op jit(solution)/shard_map/ppermute | solution.py:18
  13.2 0.0 copy-done.1
  13.2 0.0 copy-done.2
  13.2 0.1 shard_map.68.own_ref.pair_ref
  13.3 8.2 %collective-permute-start = (bf16[528,512]{1,0:T(8,128)(2,1)S(1)}, bf16[528,512]{1,0:T(8,128)(2,1)S(1)}, u32[]{:S(2)}, u32[]{:S(2)}) collective-permute-start(bf16[528,512]{1,0:T(8,128)(2,1)S(1)} %shard_map.68.own_ref.pair_ref), channel_id=1, source_target_pairs={{0,992},{32,0},{64,32},{96,64},{128,96},{160,128},{192,160},{224,1... | collective-permute-start | bytes 1622024 | tf_op jit(solution)/shard_map/ppermute | solution.py:18
  21.5 3.9 %collective-permute-start.4 = (bf16[528,512]{1,0:T(8,128)(2,1)S(1)}, bf16[528,512]{1,0:T(8,128)(2,1)}, u32[]{:S(2)}, u32[]{:S(2)}) collective-permute-start(bf16[528,512]{1,0:T(8,128)(2,1)S(1)} %shard_map.69.pair_ref.own_ref), channel_id=1, source_target_pairs={{0,1},{1,2},{2,3},{3,4},{4,5},{5,6},{6,7},{7,8},{8,9},{9,10},{10,1... | collective-permute-start | bytes 1622024 | tf_op jit(solution)/shard_map/ppermute | solution.py:18
  25.4 1.9 %collective-permute-start.5 = (bf16[528,512]{1,0:T(8,128)(2,1)S(1)}, bf16[528,512]{1,0:T(8,128)(2,1)S(1)}, u32[]{:S(2)}, u32[]{:S(2)}) collective-permute-start(bf16[528,512]{1,0:T(8,128)(2,1)S(1)} %shard_map.68.own_ref.pair_ref), channel_id=1, source_target_pairs={{0,31},{1,0},{2,1},{3,2},{4,3},{5,4},{6,5},{7,6},{8,7},{9,8},{10,9... | collective-permute-start | bytes 1622024 | tf_op jit(solution)/shard_map/ppermute | solution.py:18
  27.9 0.0 copy-start.4
  28.0 0.1 copy.11.stat_ref
  28.1 0.5 copy-done.4
  28.6 0.1 copy.8.stat_ref
  28.8 1.0 %shard_map.70.total_ref = f32[512,512]{1,0:T(8,128)S(1)} custom-call(f32[1,1]{1,0:T(1,128)} %bitcast.5.factor_ref, bf16[528,512]{1,0:T(8,128)(2,1)S(1)} %shard_map.68.own_ref.pair_ref, f32[512,1]{1,0:T(8,128)S(1)} %copy.11.stat_ref, bf16[528,512]{1,0:T(8,128)(2,1)S(1)} %shard_map.69.pair_ref.own_ref), custom_call_target="tpu_custom_call" | custom-call | flops 536870912 | bytes 536870 | tf_op jit(solution)/shard_map/pallas_call | solution.py:115
  29.8 1.0 %shard_map.71.total_ref = f32[512,512]{1,0:T(8,128)S(1)} custom-call(f32[1,1]{1,0:T(1,128)} %bitcast.6.factor_ref, bf16[528,512]{1,0:T(8,128)(2,1)S(1)} %shard_map.69.pair_ref.own_ref, f32[512,1]{1,0:T(8,128)S(1)} %copy.8.stat_ref, bf16[528,512]{1,0:T(8,128)(2,1)S(1)} %shard_map.68.own_ref.pair_ref), custom_call_target="tpu_custom_call" | custom-call | flops 536870912 | bytes 536870 | tf_op jit(solution)/shard_map/pallas_call | solution.py:115
  30.9 25.4 %collective-permute-done.2.other_ref = bf16[528,512]{1,0:T(8,128)(2,1)S(1)} collective-permute-done((bf16[528,512]{1,0:T(8,128)(2,1)S(1)}, bf16[528,512]{1,0:T(8,128)(2,1)S(1)}, u32[]{:S(2)}, u32[]{:S(2)}) %collective-permute-start.2) | collective-permute-done | bytes 540704 | tf_op jit(solution)/shard_map/ppermute | solution.py:18
  56.2 14.2 %collective-permute-start.3 = (bf16[528,512]{1,0:T(8,128)(2,1)S(1)}, bf16[528,512]{1,0:T(8,128)(2,1)S(1)}, u32[]{:S(2)}, u32[]{:S(2)}) collective-permute-start(bf16[528,512]{1,0:T(8,128)(2,1)S(1)} %collective-permute-done.2.other_ref), channel_id=1, source_target_pairs={{0,1},{1,2},{2,3},{3,4},{4,5},{5,6},{6,7},{7,8},{8,9},{9,10},{10,1... | collective-permute-start | bytes 1622024 | tf_op jit(solution)/shard_map/ppermute | solution.py:18
  70.4 6.1 %collective-permute-done.other_ref = bf16[528,512]{1,0:T(8,128)(2,1)S(1)} collective-permute-done((bf16[528,512]{1,0:T(8,128)(2,1)S(1)}, bf16[528,512]{1,0:T(8,128)(2,1)S(1)}, u32[]{:S(2)}, u32[]{:S(2)}) %collective-permute-start) | collective-permute-done | bytes 540704 | tf_op jit(solution)/shard_map/ppermute | solution.py:18
  76.5 3.4 %collective-permute-start.1 = (bf16[528,512]{1,0:T(8,128)(2,1)S(1)}, bf16[528,512]{1,0:T(8,128)(2,1)S(1)}, u32[]{:S(2)}, u32[]{:S(2)}) collective-permute-start(bf16[528,512]{1,0:T(8,128)(2,1)S(1)} %collective-permute-done.other_ref), channel_id=1, source_target_pairs={{0,31},{1,0},{2,1},{3,2},{4,3},{5,4},{6,5},{7,6},{8,7},{9,8},{10,9... | collective-permute-start | bytes 1622024 | tf_op jit(solution)/shard_map/ppermute | solution.py:18
  80.0 0.0 collective-permute-done.4.other_ref
  80.0 2.1 %shard_map.72.total_ref = f32[512,512]{1,0:T(8,128)S(1)} custom-call(f32[1,1]{1,0:T(1,128)} %bitcast.7.factor_ref, bf16[528,512]{1,0:T(8,128)(2,1)S(1)} %shard_map.68.own_ref.pair_ref, f32[512,1]{1,0:T(8,128)S(1)} %copy.11.stat_ref, bf16[528,512]{1,0:T(8,128)(2,1)} %collective-permute-done.4.other_ref, f32[512,512]{1,0:T(8,128)S(1)} %shard_map.70.total_ref), custom_call_target="tpu_custom_call" | custom-call | flops 536870912 | bytes 536870 | tf_op jit(solution)/shard_map/pallas_call | solution.py:115
  82.1 1.0 %shard_map.73.total_ref = f32[512,512]{1,0:T(8,128)S(1)} custom-call(f32[1,1]{1,0:T(1,128)} %bitcast.8.factor_ref, bf16[528,512]{1,0:T(8,128)(2,1)S(1)} %shard_map.68.own_ref.pair_ref, f32[512,1]{1,0:T(8,128)S(1)} %copy.11.stat_ref, bf16[528,512]{1,0:T(8,128)(2,1)S(1)} %collective-permute-done.2.other_ref, f32[512,512]{1,0:T(8,128)S(1)} %shard_map.72.total_ref), custom_call_target="tpu_custom_call" | custom-call | flops 536870912 | bytes 536870 | tf_op jit(solution)/shard_map/pallas_call | solution.py:115
  83.1 0.0 collective-permute-done.5.other_ref
  83.1 1.0 %shard_map.75.total_ref = f32[512,512]{1,0:T(8,128)S(1)} custom-call(f32[1,1]{1,0:T(1,128)} %bitcast.10.factor_ref, bf16[528,512]{1,0:T(8,128)(2,1)S(1)} %shard_map.69.pair_ref.own_ref, f32[512,1]{1,0:T(8,128)S(1)} %copy.8.stat_ref, bf16[528,512]{1,0:T(8,128)(2,1)S(1)} %collective-permute-done.5.other_ref, f32[512,512]{1,0:T(8,128)S(1)} %shard_map.71.total_ref), custom_call_target="tpu_custom_call" | custom-call | flops 536870912 | bytes 536870 | tf_op jit(solution)/shard_map/pallas_call | solution.py:115
  84.2 1.0 %shard_map.76.total_ref = f32[512,512]{1,0:T(8,128)S(1)} custom-call(f32[1,1]{1,0:T(1,128)} %bitcast.11.factor_ref, bf16[528,512]{1,0:T(8,128)(2,1)S(1)} %shard_map.69.pair_ref.own_ref, f32[512,1]{1,0:T(8,128)S(1)} %copy.8.stat_ref, bf16[528,512]{1,0:T(8,128)(2,1)S(1)} %collective-permute-done.other_ref, f32[512,512]{1,0:T(8,128)S(1)} %shard_map.75.total_ref), custom_call_target="tpu_custom_call" | custom-call | flops 536870912 | bytes 536870 | tf_op jit(solution)/shard_map/pallas_call | solution.py:115
  85.2 0.0 collective-permute-done.3.both_ref
  85.2 1.9 %shard_map.74 = f32[512,512]{1,0:T(8,128)} custom-call(f32[1,1]{1,0:T(1,128)} %bitcast.9.factor_ref, bf16[528,512]{1,0:T(8,128)(2,1)S(1)} %shard_map.68.own_ref.pair_ref, f32[512,1]{1,0:T(8,128)S(1)} %copy.11.stat_ref, bf16[528,512]{1,0:T(8,128)(2,1)S(1)} %collective-permute-done.3.both_ref, f32[512,512]{1,0:T(8,128)S(1)} %shard_map.73.total_ref), custom_call_target="tpu_custom_call" | custom-call | flops 536870912 | bytes 536870 | tf_op jit(solution)/shard_map/pallas_call | solution.py:115
  87.1 2.2 %collective-permute-done.1.both_ref = bf16[528,512]{1,0:T(8,128)(2,1)S(1)} collective-permute-done((bf16[528,512]{1,0:T(8,128)(2,1)S(1)}, bf16[528,512]{1,0:T(8,128)(2,1)S(1)}, u32[]{:S(2)}, u32[]{:S(2)}) %collective-permute-start.1) | collective-permute-done | bytes 540704 | tf_op jit(solution)/shard_map/ppermute | solution.py:18
  89.3 1.9 %shard_map.77 = f32[512,512]{1,0:T(8,128)} custom-call(f32[1,1]{1,0:T(1,128)} %bitcast.12.factor_ref, bf16[528,512]{1,0:T(8,128)(2,1)S(1)} %shard_map.69.pair_ref.own_ref, f32[512,1]{1,0:T(8,128)S(1)} %copy.8.stat_ref, bf16[528,512]{1,0:T(8,128)(2,1)S(1)} %collective-permute-done.1.both_ref, f32[512,512]{1,0:T(8,128)S(1)} %shard_map.76.total_ref), custom_call_target="tpu_custom_call" | custom-call | flops 536870912 | bytes 536870 | tf_op jit(solution)/shard_map/pallas_call | solution.py:115
Async XLA Ops:
  0.6 1.0 %copy-start = (bf16[512,512]{1,0:T(8,128)(2,1)S(1)}, bf16[512,512]{1,0:T(8,128)(2,1)}, u32[]{:S(2)}) copy-start(bf16[512,512]{1,0:T(8,128)(2,1)} %rows_ref.3) | copy-start | bytes 1572868
  1.7 0.7 copy-start.3
  2.4 10.9 %copy-start.1 = (bf16[512,512]{1,0:T(8,128)(2,1)S(1)}, bf16[512,512]{1,0:T(8,128)(2,1)}, u32[]{:S(2)}) copy-start(bf16[512,512]{1,0:T(8,128)(2,1)} %rows_ref.2) | copy-start | bytes 1572868
  2.4 10.9 %copy-start.2 = (f32[512]{0:T(512)S(1)}, f32[512]{0:T(512)}, u32[]{:S(2)}) copy-start(f32[512]{0:T(512)} %param.7) | copy-start | bytes 6148
  2.4 53.8 %collective-permute-start.2 = (bf16[528,512]{1,0:T(8,128)(2,1)S(1)}, bf16[528,512]{1,0:T(8,128)(2,1)S(1)}, u32[]{:S(2)}, u32[]{:S(2)}) collective-permute-start(bf16[528,512]{1,0:T(8,128)(2,1)S(1)} %shard_map.69.pair_ref.own_ref), channel_id=1, source_target_pairs={{0,32},{32,64},{64,96},{96,128},{128,160},{160,192},{192,224},{224... | collective-permute-start | bytes 1622024 | tf_op jit(solution)/shard_map/ppermute | solution.py:18
  13.3 63.2 %collective-permute-start = (bf16[528,512]{1,0:T(8,128)(2,1)S(1)}, bf16[528,512]{1,0:T(8,128)(2,1)S(1)}, u32[]{:S(2)}, u32[]{:S(2)}) collective-permute-start(bf16[528,512]{1,0:T(8,128)(2,1)S(1)} %shard_map.68.own_ref.pair_ref), channel_id=1, source_target_pairs={{0,992},{32,0},{64,32},{96,64},{128,96},{160,128},{192,160},{224,1... | collective-permute-start | bytes 1622024 | tf_op jit(solution)/shard_map/ppermute | solution.py:18
  21.5 58.5 %collective-permute-start.4 = (bf16[528,512]{1,0:T(8,128)(2,1)S(1)}, bf16[528,512]{1,0:T(8,128)(2,1)}, u32[]{:S(2)}, u32[]{:S(2)}) collective-permute-start(bf16[528,512]{1,0:T(8,128)(2,1)S(1)} %shard_map.69.pair_ref.own_ref), channel_id=1, source_target_pairs={{0,1},{1,2},{2,3},{3,4},{4,5},{5,6},{6,7},{7,8},{8,9},{9,10},{10,1... | collective-permute-start | bytes 1622024 | tf_op jit(solution)/shard_map/ppermute | solution.py:18
  25.4 57.8 %collective-permute-start.5 = (bf16[528,512]{1,0:T(8,128)(2,1)S(1)}, bf16[528,512]{1,0:T(8,128)(2,1)S(1)}, u32[]{:S(2)}, u32[]{:S(2)}) collective-permute-start(bf16[528,512]{1,0:T(8,128)(2,1)S(1)} %shard_map.68.own_ref.pair_ref), channel_id=1, source_target_pairs={{0,31},{1,0},{2,1},{3,2},{4,3},{5,4},{6,5},{7,6},{8,7},{9,8},{10,9... | collective-permute-start | bytes 1622024 | tf_op jit(solution)/shard_map/ppermute | solution.py:18
  27.9 0.7 copy-start.4
  56.2 29.0 %collective-permute-start.3 = (bf16[528,512]{1,0:T(8,128)(2,1)S(1)}, bf16[528,512]{1,0:T(8,128)(2,1)S(1)}, u32[]{:S(2)}, u32[]{:S(2)}) collective-permute-start(bf16[528,512]{1,0:T(8,128)(2,1)S(1)} %collective-permute-done.2.other_ref), channel_id=1, source_target_pairs={{0,1},{1,2},{2,3},{3,4},{4,5},{5,6},{6,7},{7,8},{8,9},{9,10},{10,1... | collective-permute-start | bytes 1622024 | tf_op jit(solution)/shard_map/ppermute | solution.py:18
  76.5 12.8 %collective-permute-start.1 = (bf16[528,512]{1,0:T(8,128)(2,1)S(1)}, bf16[528,512]{1,0:T(8,128)(2,1)S(1)}, u32[]{:S(2)}, u32[]{:S(2)}) collective-permute-start(bf16[528,512]{1,0:T(8,128)(2,1)S(1)} %collective-permute-done.other_ref), channel_id=1, source_target_pairs={{0,31},{1,0},{2,1},{3,2},{4,3},{5,4},{6,5},{7,6},{8,7},{9,8},{10,9... | collective-permute-start | bytes 1622024 | tf_op jit(solution)/shard_map/ppermute | solution.py:18

commit v6 on v4

--- a/solution.py
+++ b/solution.py
@@ -8,7 +8,8 @@
 STAT_ROWS = 16
 BLOCKS = 2
 VMEM_BYTES = 16 * 1024 * 1024
-PACK_VMEM_BYTES = 8 * 1024 * 1024
+PIECES = 4
+PACK_VMEM_BYTES = 60 * 1024 * 1024
 COSTS = (2**29, 2**29, 2**29, 2**29)
 
 
@@ -18,31 +19,50 @@
     return lax.ppermute(value, axis, pairs)
 
 
-def pack_kernel(rows_ref, stat_ref, out, sem):
+def pack_kernel(rows_ref, stat_ref, out, held, sems):
     rows = rows_ref.shape[0]
-    copy = pltpu.make_async_copy(rows_ref, out.at[pl.ds(0, rows), :], sem)
-    copy.start()
+    size = rows // PIECES
+    cuts = [pl.ds(k * size, size) for k in range(PIECES)]
+    loads = [
+        pltpu.make_async_copy(rows_ref.at[cut, :], held.at[cut, :], sems.at[0, k])
+        for k, cut in enumerate(cuts)
+    ]
+    cuts.append(pl.ds(rows, STAT_ROWS))
+    stores = [
+        pltpu.make_async_copy(held.at[cut, :], out.at[cut, :], sems.at[1, k])
+        for k, cut in enumerate(cuts)
+    ]
+    for load in loads:
+        load.start()
     stat = stat_ref[...]
     upper = stat.astype(jnp.bfloat16).astype(jnp.float32)
     rest = stat - upper
     middle = rest.astype(jnp.bfloat16).astype(jnp.float32)
     lower = rest - middle
     zeros = jnp.zeros((STAT_ROWS - 3, stat.shape[1]), jnp.float32)
-    out[pl.ds(rows, STAT_ROWS), :] = jnp.concatenate(
+    held[pl.ds(rows, STAT_ROWS), :] = jnp.concatenate(
         [upper, middle, lower, zeros], axis=0
     ).astype(jnp.bfloat16)
-    copy.wait()
+    stores[PIECES].start()
+    for k in range(PIECES):
+        loads[k].wait()
+        stores[k].start()
+    for store in stores:
+        store.wait()
 
 
 def pack(block, stat):
     rows, width = block.shape
-    vmem = pl.BlockSpec(memory_space=pltpu.VMEM)
+    hbm = pl.BlockSpec(memory_space=pltpu.HBM)
     return pl.pallas_call(
         pack_kernel,
-        in_specs=[pl.BlockSpec(memory_space=pltpu.HBM), vmem],
-        out_specs=vmem,
+        in_specs=[hbm, pl.BlockSpec(memory_space=pltpu.VMEM)],
+        out_specs=hbm,
         out_shape=jax.ShapeDtypeStruct((rows + STAT_ROWS, width), jnp.bfloat16),
-        scratch_shapes=[pltpu.SemaphoreType.DMA],
+        scratch_shapes=[
+            pltpu.VMEM((rows + STAT_ROWS, width), jnp.bfloat16),
+            pltpu.SemaphoreType.DMA((2, PIECES + 1)),
+        ],
         compiler_params=pltpu.CompilerParams(vmem_limit_bytes=PACK_VMEM_BYTES),
     )(block, stat.reshape(1, rows))
 

time: 91.6 us -> 95.1 us (1.038)
  the two profiles are of different devices: /device:TPU:183 before, /device:TPU:175 now
where the time goes in v6:
time: 95.1 us; the launch traced here: 94.6 us
  starting transfers between devices  44.2 us (46%)
  waiting for transfers between devices  32 us (34%)
  Pallas kernels  15 us (16%)
  local copies, waits for them, and re-layouts  1.88 us (2%)
  between operations  1.5 us (2%)
    ppermute x6, starting transfers between devices, shifted(): return lax.ppermute(value, axis, pairs)  44.2 us
    ppermute x6, waiting for transfers between devices, shifted(): return lax.ppermute(value, axis, pairs)  32 us
    pallas_call x8, Pallas kernels, call(): pl.pallas_call(kernel, in_specs=[pl.BlockSpec(memory_space=pltpu.SMEM)] +...  9.97 us
    pallas_call x2, Pallas kernels, pack(): pl.pallas_call(pack_kernel, in_specs=[hbm, pl.BlockSpec(memory_space=pltp...  5.06 us
  transfers between devices with their start and end apart: 6, of which 3 were waited for; matrix products, arithmetic and copies ran while one was open for 0% of the time, Pallas kernels for 11%

profile of v6, /device:TPU:175, one launch (start us, length us, event | category | flops | bytes accessed | tf_op | source)
XLA Modules:
  0.0 94.6 jit_solution(3314233608282045392)
XLA Ops:
  0.6 2.5 %shard_map.69.pair_ref.own_ref = bf16[528,512]{1,0:T(8,128)(2,1)} custom-call(bf16[512,512]{1,0:T(8,128)(2,1)} %rows_ref.3, f32[1,512]{1,0:T(1,128)} %bitcast.15), custom_call_target="tpu_custom_call" | custom-call | tf_op jit(solution)/shard_map/pallas_call | solution.py:57
  3.2 0.0 copy-start
  3.2 10.8 %collective-permute-start.1 = (bf16[528,512]{1,0:T(8,128)(2,1)}, bf16[528,512]{1,0:T(8,128)(2,1)S(1)}, u32[]{:S(2)}, u32[]{:S(2)}) collective-permute-start(bf16[528,512]{1,0:T(8,128)(2,1)} %shard_map.69.pair_ref.own_ref), channel_id=1, source_target_pairs={{0,32},{32,64},{64,96},{96,128},{128,160},{160,192},{192,224},{224... | collective-permute-start | bytes 1622024 | tf_op jit(solution)/shard_map/ppermute | solution.py:19
  14.0 2.5 %shard_map.68.own_ref.pair_ref = bf16[528,512]{1,0:T(8,128)(2,1)} custom-call(bf16[512,512]{1,0:T(8,128)(2,1)} %rows_ref.2, f32[1,512]{1,0:T(1,128)} %bitcast.13), custom_call_target="tpu_custom_call" | custom-call | tf_op jit(solution)/shard_map/pallas_call | solution.py:57
  16.5 0.0 copy-start.3
  16.5 8.2 %collective-permute-start = (bf16[528,512]{1,0:T(8,128)(2,1)}, bf16[528,512]{1,0:T(8,128)(2,1)S(1)}, u32[]{:S(2)}, u32[]{:S(2)}) collective-permute-start(bf16[528,512]{1,0:T(8,128)(2,1)} %shard_map.68.own_ref.pair_ref), channel_id=1, source_target_pairs={{0,992},{32,0},{64,32},{96,64},{128,96},{160,128},{192,160},{224,1... | collective-permute-start | bytes 1622024 | tf_op jit(solution)/shard_map/ppermute | solution.py:19
  24.7 2.9 %collective-permute-start.5 = (bf16[528,512]{1,0:T(8,128)(2,1)}, bf16[528,512]{1,0:T(8,128)(2,1)S(1)}, u32[]{:S(2)}, u32[]{:S(2)}) collective-permute-start(bf16[528,512]{1,0:T(8,128)(2,1)} %shard_map.68.own_ref.pair_ref), channel_id=1, source_target_pairs={{0,31},{1,0},{2,1},{3,2},{4,3},{5,4},{6,5},{7,6},{8,7},{9,8},{10,9... | collective-permute-start | bytes 1622024 | tf_op jit(solution)/shard_map/ppermute | solution.py:19
  27.6 0.0 copy-done
  27.6 4.8 %collective-permute-start.4 = (bf16[528,512]{1,0:T(8,128)(2,1)S(1)}, bf16[528,512]{1,0:T(8,128)(2,1)S(1)}, u32[]{:S(2)}, u32[]{:S(2)}) collective-permute-start(bf16[528,512]{1,0:T(8,128)(2,1)S(1)} %copy-done), channel_id=1, source_target_pairs={{0,1},{1,2},{2,3},{3,4},{4,5},{5,6},{6,7},{7,8},{8,9},{9,10},{10,1... | collective-permute-start | bytes 1622024 | tf_op jit(solution)/shard_map/ppermute | solution.py:19
  33.0 0.0 copy-done.3
  33.0 0.0 copy-start.4
  33.1 0.1 copy.8.stat_ref
  33.2 0.5 copy-done.4
  33.7 0.1 copy.9.stat_ref
  33.9 0.0 copy-start.1
  33.9 1.0 %copy-done.1 = bf16[528,512]{1,0:T(8,128)(2,1)S(1)} copy-done((bf16[528,512]{1,0:T(8,128)(2,1)S(1)}, bf16[528,512]{1,0:T(8,128)(2,1)}, u32[]{:S(2)}) %copy-start.1) | copy-done | bytes 540696
  34.9 1.0 %shard_map.70.total_ref = f32[512,512]{1,0:T(8,128)S(1)} custom-call(f32[1,1]{1,0:T(1,128)} %bitcast.5.factor_ref, bf16[528,512]{1,0:T(8,128)(2,1)S(1)} %copy-done.1, f32[512,1]{1,0:T(8,128)S(1)} %copy.8.stat_ref, bf16[528,512]{1,0:T(8,128)(2,1)S(1)} %copy-done), custom_call_target="tpu_custom_call" | custom-call | flops 536870912 | bytes 536870 | tf_op jit(solution)/shard_map/pallas_call | solution.py:135
  36.0 0.0 copy-start.2
  36.0 1.0 %shard_map.72.total_ref = f32[512,512]{1,0:T(8,128)S(1)} custom-call(f32[1,1]{1,0:T(1,128)} %bitcast.7.factor_ref, bf16[528,512]{1,0:T(8,128)(2,1)S(1)} %copy-done, f32[512,1]{1,0:T(8,128)S(1)} %copy.9.stat_ref, bf16[528,512]{1,0:T(8,128)(2,1)S(1)} %copy-done.1), custom_call_target="tpu_custom_call" | custom-call | flops 536870912 | bytes 536870 | tf_op jit(solution)/shard_map/pallas_call | solution.py:135
  37.0 20.1 %collective-permute-done.1.other_ref = bf16[528,512]{1,0:T(8,128)(2,1)S(1)} collective-permute-done((bf16[528,512]{1,0:T(8,128)(2,1)}, bf16[528,512]{1,0:T(8,128)(2,1)S(1)}, u32[]{:S(2)}, u32[]{:S(2)}) %collective-permute-start.1) | collective-permute-done | bytes 540704 | tf_op jit(solution)/shard_map/ppermute | solution.py:19
  57.2 14.2 %collective-permute-start.3 = (bf16[528,512]{1,0:T(8,128)(2,1)S(1)}, bf16[528,512]{1,0:T(8,128)(2,1)S(1)}, u32[]{:S(2)}, u32[]{:S(2)}) collective-permute-start(bf16[528,512]{1,0:T(8,128)(2,1)S(1)} %collective-permute-done.1.other_ref), channel_id=1, source_target_pairs={{0,1},{1,2},{2,3},{3,4},{4,5},{5,6},{6,7},{7,8},{8,9},{9,10},{10,1... | collective-permute-start | bytes 1622024 | tf_op jit(solution)/shard_map/ppermute | solution.py:19
  71.4 0.0 copy-done.2
  71.4 1.0 %shard_map.71.total_ref = f32[512,512]{1,0:T(8,128)S(1)} custom-call(f32[1,1]{1,0:T(1,128)} %bitcast.6.factor_ref, bf16[528,512]{1,0:T(8,128)(2,1)S(1)} %copy-done.2, f32[512,1]{1,0:T(8,128)S(1)} %copy.8.stat_ref, bf16[528,512]{1,0:T(8,128)(2,1)S(1)} %collective-permute-done.1.other_ref, f32[512,512]{1,0:T(8,128)S(1)} %shard_map.70.total_ref), custom_call_target="tpu_custom_call" | custom-call | flops 536870912 | bytes 536870 | tf_op jit(solution)/shard_map/pallas_call | solution.py:135
  72.4 7.5 %collective-permute-done.other_ref = bf16[528,512]{1,0:T(8,128)(2,1)S(1)} collective-permute-done((bf16[528,512]{1,0:T(8,128)(2,1)}, bf16[528,512]{1,0:T(8,128)(2,1)S(1)}, u32[]{:S(2)}, u32[]{:S(2)}) %collective-permute-start) | collective-permute-done | bytes 540704 | tf_op jit(solution)/shard_map/ppermute | solution.py:19
  79.9 3.4 %collective-permute-start.2 = (bf16[528,512]{1,0:T(8,128)(2,1)S(1)}, bf16[528,512]{1,0:T(8,128)(2,1)S(1)}, u32[]{:S(2)}, u32[]{:S(2)}) collective-permute-start(bf16[528,512]{1,0:T(8,128)(2,1)S(1)} %collective-permute-done.other_ref), channel_id=1, source_target_pairs={{0,31},{1,0},{2,1},{3,2},{4,3},{5,4},{6,5},{7,6},{8,7},{9,8},{10,9... | collective-permute-start | bytes 1622024 | tf_op jit(solution)/shard_map/ppermute | solution.py:19
  83.4 0.0 collective-permute-done.5.other_ref
  83.4 1.0 %shard_map.75.total_ref = f32[512,512]{1,0:T(8,128)S(1)} custom-call(f32[1,1]{1,0:T(1,128)} %bitcast.10.factor_ref, bf16[528,512]{1,0:T(8,128)(2,1)S(1)} %copy-done, f32[512,1]{1,0:T(8,128)S(1)} %copy.9.stat_ref, bf16[528,512]{1,0:T(8,128)(2,1)S(1)} %collective-permute-done.5.other_ref, f32[512,512]{1,0:T(8,128)S(1)} %shard_map.72.total_ref), custom_call_target="tpu_custom_call" | custom-call | flops 536870912 | bytes 536870 | tf_op jit(solution)/shard_map/pallas_call | solution.py:135
  84.4 1.0 %shard_map.76.total_ref = f32[512,512]{1,0:T(8,128)S(1)} custom-call(f32[1,1]{1,0:T(1,128)} %bitcast.11.factor_ref, bf16[528,512]{1,0:T(8,128)(2,1)S(1)} %copy-done, f32[512,1]{1,0:T(8,128)S(1)} %copy.9.stat_ref, bf16[528,512]{1,0:T(8,128)(2,1)S(1)} %collective-permute-done.other_ref, f32[512,512]{1,0:T(8,128)S(1)} %shard_map.75.total_ref), custom_call_target="tpu_custom_call" | custom-call | flops 536870912 | bytes 536870 | tf_op jit(solution)/shard_map/pallas_call | solution.py:135
  85.5 0.0 collective-permute-done.4.other_ref
  85.5 1.0 %shard_map.73.total_ref = f32[512,512]{1,0:T(8,128)S(1)} custom-call(f32[1,1]{1,0:T(1,128)} %bitcast.8.factor_ref, bf16[528,512]{1,0:T(8,128)(2,1)S(1)} %copy-done.2, f32[512,1]{1,0:T(8,128)S(1)} %copy.8.stat_ref, bf16[528,512]{1,0:T(8,128)(2,1)S(1)} %collective-permute-done.4.other_ref, f32[512,512]{1,0:T(8,128)S(1)} %shard_map.71.total_ref), custom_call_target="tpu_custom_call" | custom-call | flops 536870912 | bytes 536870 | tf_op jit(solution)/shard_map/pallas_call | solution.py:135
  86.5 0.0 collective-permute-done.3.both_ref
  86.5 1.9 %shard_map.74 = f32[512,512]{1,0:T(8,128)} custom-call(f32[1,1]{1,0:T(1,128)} %bitcast.9.factor_ref, bf16[528,512]{1,0:T(8,128)(2,1)S(1)} %copy-done.2, f32[512,1]{1,0:T(8,128)S(1)} %copy.8.stat_ref, bf16[528,512]{1,0:T(8,128)(2,1)S(1)} %collective-permute-done.3.both_ref, f32[512,512]{1,0:T(8,128)S(1)} %shard_map.73.total_ref), custom_call_target="tpu_custom_call" | custom-call | flops 536870912 | bytes 536870 | tf_op jit(solution)/shard_map/pallas_call | solution.py:135
  88.4 4.3 %collective-permute-done.2.both_ref = bf16[528,512]{1,0:T(8,128)(2,1)S(1)} collective-permute-done((bf16[528,512]{1,0:T(8,128)(2,1)S(1)}, bf16[528,512]{1,0:T(8,128)(2,1)S(1)}, u32[]{:S(2)}, u32[]{:S(2)}) %collective-permute-start.2) | collective-permute-done | bytes 540704 | tf_op jit(solution)/shard_map/ppermute | solution.py:19
  92.7 1.9 %shard_map.77 = f32[512,512]{1,0:T(8,128)} custom-call(f32[1,1]{1,0:T(1,128)} %bitcast.12.factor_ref, bf16[528,512]{1,0:T(8,128)(2,1)S(1)} %copy-done, f32[512,1]{1,0:T(8,128)S(1)} %copy.9.stat_ref, bf16[528,512]{1,0:T(8,128)(2,1)S(1)} %collective-permute-done.2.both_ref, f32[512,512]{1,0:T(8,128)S(1)} %shard_map.76.total_ref), custom_call_target="tpu_custom_call" | custom-call | flops 536870912 | bytes 536870 | tf_op jit(solution)/shard_map/pallas_call | solution.py:135
Async XLA Ops:
  3.2 24.4 %copy-start = (bf16[528,512]{1,0:T(8,128)(2,1)S(1)}, bf16[528,512]{1,0:T(8,128)(2,1)}, u32[]{:S(2)}) copy-start(bf16[528,512]{1,0:T(8,128)(2,1)} %shard_map.69.pair_ref.own_ref) | copy-start | bytes 1622020
  3.2 54.0 %collective-permute-start.1 = (bf16[528,512]{1,0:T(8,128)(2,1)}, bf16[528,512]{1,0:T(8,128)(2,1)S(1)}, u32[]{:S(2)}, u32[]{:S(2)}) collective-permute-start(bf16[528,512]{1,0:T(8,128)(2,1)} %shard_map.69.pair_ref.own_ref), channel_id=1, source_target_pairs={{0,32},{32,64},{64,96},{96,128},{128,160},{160,192},{192,224},{224... | collective-permute-start | bytes 1622024 | tf_op jit(solution)/shard_map/ppermute | solution.py:19
  16.5 16.6 %copy-start.3 = (f32[512]{0:T(512)S(1)}, f32[512]{0:T(512)}, u32[]{:S(2)}) copy-start(f32[512]{0:T(512)} %param.7) | copy-start | bytes 6148
  16.5 63.4 %collective-permute-start = (bf16[528,512]{1,0:T(8,128)(2,1)}, bf16[528,512]{1,0:T(8,128)(2,1)S(1)}, u32[]{:S(2)}, u32[]{:S(2)}) collective-permute-start(bf16[528,512]{1,0:T(8,128)(2,1)} %shard_map.68.own_ref.pair_ref), channel_id=1, source_target_pairs={{0,992},{32,0},{64,32},{96,64},{128,96},{160,128},{192,160},{224,1... | collective-permute-start | bytes 1622024 | tf_op jit(solution)/shard_map/ppermute | solution.py:19
  24.7 58.7 %collective-permute-start.5 = (bf16[528,512]{1,0:T(8,128)(2,1)}, bf16[528,512]{1,0:T(8,128)(2,1)S(1)}, u32[]{:S(2)}, u32[]{:S(2)}) collective-permute-start(bf16[528,512]{1,0:T(8,128)(2,1)} %shard_map.68.own_ref.pair_ref), channel_id=1, source_target_pairs={{0,31},{1,0},{2,1},{3,2},{4,3},{5,4},{6,5},{7,6},{8,7},{9,8},{10,9... | collective-permute-start | bytes 1622024 | tf_op jit(solution)/shard_map/ppermute | solution.py:19
  27.6 57.9 %collective-permute-start.4 = (bf16[528,512]{1,0:T(8,128)(2,1)S(1)}, bf16[528,512]{1,0:T(8,128)(2,1)S(1)}, u32[]{:S(2)}, u32[]{:S(2)}) collective-permute-start(bf16[528,512]{1,0:T(8,128)(2,1)S(1)} %copy-done), channel_id=1, source_target_pairs={{0,1},{1,2},{2,3},{3,4},{4,5},{5,6},{6,7},{7,8},{8,9},{9,10},{10,1... | collective-permute-start | bytes 1622024 | tf_op jit(solution)/shard_map/ppermute | solution.py:19
  33.0 0.7 copy-start.4
  33.9 1.1 %copy-start.1 = (bf16[528,512]{1,0:T(8,128)(2,1)S(1)}, bf16[528,512]{1,0:T(8,128)(2,1)}, u32[]{:S(2)}) copy-start(bf16[528,512]{1,0:T(8,128)(2,1)} %shard_map.68.own_ref.pair_ref) | copy-start | bytes 1622020
  36.0 35.4 %copy-start.2 = (bf16[528,512]{1,0:T(8,128)(2,1)S(1)}, bf16[528,512]{1,0:T(8,128)(2,1)}, u32[]{:S(2)}) copy-start(bf16[528,512]{1,0:T(8,128)(2,1)} %shard_map.68.own_ref.pair_ref) | copy-start | bytes 1622020
  57.2 29.4 %collective-permute-start.3 = (bf16[528,512]{1,0:T(8,128)(2,1)S(1)}, bf16[528,512]{1,0:T(8,128)(2,1)S(1)}, u32[]{:S(2)}, u32[]{:S(2)}) collective-permute-start(bf16[528,512]{1,0:T(8,128)(2,1)S(1)} %collective-permute-done.1.other_ref), channel_id=1, source_target_pairs={{0,1},{1,2},{2,3},{3,4},{4,5},{5,6},{6,7},{7,8},{8,9},{9,10},{10,1... | collective-permute-start | bytes 1622024 | tf_op jit(solution)/shard_map/ppermute | solution.py:19
  79.9 12.8 %collective-permute-start.2 = (bf16[528,512]{1,0:T(8,128)(2,1)S(1)}, bf16[528,512]{1,0:T(8,128)(2,1)S(1)}, u32[]{:S(2)}, u32[]{:S(2)}) collective-permute-start(bf16[528,512]{1,0:T(8,128)(2,1)S(1)} %collective-permute-done.other_ref), channel_id=1, source_target_pairs={{0,31},{1,0},{2,1},{3,2},{4,3},{5,4},{6,5},{7,6},{8,7},{9,8},{10,9... | collective-permute-start | bytes 1622024 | tf_op jit(solution)/shard_map/ppermute | solution.py:19
